TPU v7x, 32 devices: a whole 2x2x4 slice. The times are simulated.
32 devices in a mesh: row: 4 (over y, x), col: 8 (over z, core).
Axes of the slice: x: 2, y: 2, z: 4, core: 2. Of those that a mesh axis runs over, the one named last changes fastest.
Arguments:
- affinity: bfloat16 [4, 8, 16, 256, 256], P('row', 'col'), may hold values from 9e-05 to 32.4
- block_rows: int32 [4, 8, 16], P('row', 'col'), may hold values from 0 to 3, as said below
- block_cols: int32 [4, 8, 16], P('row', 'col'), may hold values from 0 to 7
- block_count: int32 [4, 8], P('row', 'col'), may hold values from 4 to 16, as said below
- labels: float32 [8192, 1024], P(('row', 'col')), may hold values from 0 to 1
- labelled: int32 [8192], P(('row', 'col')), may hold values 0 or 1
Outputs:
- scores: float32 [8192, 1024], P(('row', 'col'))
Inputs may be any that keep to these rules, and one draw needn't show every extreme that they name: Within one entry (r, c) the pairs (block_rows, block_cols) of all 16 slots are distinct, and its first 4 slots name every row block once. `block_count`: some entry has all 16 slots live.
All inputs are finite; a program needn't handle non-finite values. No bound on the sum of `labelled` on one device may be relied on, other than what follows from the above.
Results may differ from a plain program's by a relative error of at most 0.0003.
Values may be sent and summed in bfloat16 or wider, within the bound.
No kernel may reach another device: no remote copies, remote signals or barrier semaphores. Data moves between devices by JAX's collectives and lax.ppermute only.
A program may use at most 128 MiB of HBM per device.

v0:
```python
import jax
import jax.numpy as jnp
from jax import lax
from jax.sharding import PartitionSpec as P

SWEEPS = 2


spread_weight = 0.8


def group_term(tile_stack, row_ids, col_ids, slot_live, gathered, group_id, group_width):
    first_slot = group_id * group_width
    tile_group = lax.dynamic_slice_in_dim(tile_stack, first_slot, group_width, 0)
    group_rows = lax.dynamic_slice_in_dim(row_ids, first_slot, group_width, 0)
    group_cols = lax.dynamic_slice_in_dim(col_ids, first_slot, group_width, 0)
    group_live = lax.dynamic_slice_in_dim(slot_live, first_slot, group_width, 0)
    fetched = jnp.take(gathered, group_cols, axis=0)
    product = jnp.einsum("gij,gjc->gic", tile_group, fetched, preferred_element_type=jnp.float32)
    placing = (
        (group_rows[None, :] == jnp.arange(group_width)[:, None]) & group_live[None, :]
    ).astype(jnp.float32)
    return jnp.einsum("rg,gic->ric", placing, product, precision=lax.Precision.HIGHEST)


def on_device(affinity, block_rows, block_cols, block_count, labels, labelled):
    tile_stack = affinity[0, 0]
    row_ids = block_rows[0, 0]
    col_ids = block_cols[0, 0]
    live_count = block_count[0, 0]
    row_groups = lax.axis_size("row")
    col_groups = lax.axis_size("col")
    slot_total = tile_stack.shape[0]
    tile_rows = tile_stack.shape[1]
    classes = labels.shape[1]
    slot_live = jnp.arange(slot_total) < live_count
    placing = ((row_ids[None, :] == jnp.arange(row_groups)[:, None]) & slot_live[None, :]).astype(
        jnp.float32
    )
    row_sums = jnp.sum(tile_stack, axis=2, dtype=jnp.float32)
    degree_part = jnp.dot(placing, row_sums, precision=lax.Precision.HIGHEST)
    degree = lax.psum_scatter(degree_part, "row", scatter_dimension=0, tiled=True).reshape(
        tile_rows, 1
    )
    keep_rows = labelled[:, None] == 1
    current = labels
    group_total = slot_total // row_groups
    for iteration in range(SWEEPS):
        gathered = lax.all_gather(current.astype(jnp.bfloat16), "col", axis=0, tiled=True)
        gathered = gathered.reshape(col_groups, tile_rows, classes)

        def add_group(group_id, running):
            return running + group_term(
                tile_stack, row_ids, col_ids, slot_live, gathered, group_id, row_groups
            )

        empty = jnp.zeros((row_groups, tile_rows, classes), jnp.float32)
        running = lax.fori_loop(0, group_total, add_group, empty)
        flat_terms = running.reshape(row_groups * tile_rows, classes)
        summed = lax.psum_scatter(flat_terms, "row", scatter_dimension=0, tiled=True)
        spread = spread_weight * summed / degree + (1.0 - spread_weight) * labels
        current = jnp.where(keep_rows, labels, spread)
    return current


def solution(mesh):
    placed = (
        P("row", "col", None, None, None),
        P("row", "col", None),
        P("row", "col", None),
        P("row", "col"),
        P(("row", "col"), None),
        P(("row", "col")),
    )
    return jax.shard_map(
        on_device, mesh=mesh, in_specs=placed, out_specs=P(("row", "col"), None), check_vma=False
    )
```

profile of v0, /device:TPU:0, one launch (start us, length us, event | category | flops | bytes accessed | tf_op | source)
XLA Modules:
  0.0 390.5 jit_solution(4449040576525262673)
XLA Ops:
  9.4 49.5 %all-gather.3.cloned.1.call-done = bf16[2048,1024]{1,0:T(8,128)(2,1)} async-done(((bf16[256,1024]{1,0:T(8,128)(2,1)}), bf16[2048,1024]{1,0:T(8,128)(2,1)}) %all-gather.3.cloned.1.call-update) | async-done | bytes 4194320 | tf_op jit(solution)/shard_map/all_gather | solution.py:49
  58.8 79.3 %while.28 = (s32[]{:T(128)}, f32[4,256,1024]{2,0,1:T(4,128)}, s32[16]{0:T(128)}, pred[16]{0:T(512)(128)(4,1)S(1)}, bf16[16,256,256]{2,1,0:T(8,128)(2,1)}, /*inde...) while((s32[]{:T(128)}, f32[4,256,1024]{2,0,1:T(4,128)}, ...), condition=%wide.region_1.3_spmd.clone, body=%wide.region_0.2_spmd.clone.sunk | while | flops 590349312 | bytes 23597652 | solution.py:58
  59.6 2.9 gather_fusion
  62.5 3.8 fusion.52
  66.4 11.3 %select_add_fusion.4 = f32[4,256,1024]{2,0,1:T(4,128)} fusion(f32[4,256,1024]{2,0,1:T(4,128)} %get-tuple-element.442, f32[4,256,1024]{2,1,0:T(8,128)} %fusion.52, pred[]{:T(512)S(6)} %compare.6, s32[4]{0:T(128)S(1)} %dynamic_slice.79, pred[4]{0:T(512)(128)(4,1)S(1)} %dynamic_slice.80), kind=kOutput, calls=%fused_computation.4.clone.1 | convolution fusion | flops 52428832 | bytes 12582933 | tf_op jit(solution)/shard_map/while/body/eval_jaxpr/rg,gic->ric/dot_general | solution.py:23
  78.5 2.9 gather_fusion
  81.3 3.8 fusion.52
  85.3 12.6 %select_add_fusion.4 = f32[4,256,1024]{2,0,1:T(4,128)} fusion(f32[4,256,1024]{2,0,1:T(4,128)} %get-tuple-element.442, f32[4,256,1024]{2,1,0:T(8,128)} %fusion.52, pred[]{:T(512)S(6)} %compare.6, s32[4]{0:T(128)S(1)} %dynamic_slice.79, pred[4]{0:T(512)(128)(4,1)S(1)} %dynamic_slice.80), kind=kOutput, calls=%fused_computation.4.clone.1 | convolution fusion | flops 52428832 | bytes 12582933 | tf_op jit(solution)/shard_map/while/body/eval_jaxpr/rg,gic->ric/dot_general | solution.py:23
  98.6 2.9 gather_fusion
  101.5 3.8 fusion.52
  105.4 12.6 %select_add_fusion.4 = f32[4,256,1024]{2,0,1:T(4,128)} fusion(f32[4,256,1024]{2,0,1:T(4,128)} %get-tuple-element.442, f32[4,256,1024]{2,1,0:T(8,128)} %fusion.52, pred[]{:T(512)S(6)} %compare.6, s32[4]{0:T(128)S(1)} %dynamic_slice.79, pred[4]{0:T(512)(128)(4,1)S(1)} %dynamic_slice.80), kind=kOutput, calls=%fused_computation.4.clone.1 | convolution fusion | flops 52428832 | bytes 12582933 | tf_op jit(solution)/shard_map/while/body/eval_jaxpr/rg,gic->ric/dot_general | solution.py:23
  118.8 2.9 gather_fusion
  121.6 3.8 fusion.52
  125.6 12.6 %select_add_fusion.4 = f32[4,256,1024]{2,0,1:T(4,128)} fusion(f32[4,256,1024]{2,0,1:T(4,128)} %get-tuple-element.442, f32[4,256,1024]{2,1,0:T(8,128)} %fusion.52, pred[]{:T(512)S(6)} %compare.6, s32[4]{0:T(128)S(1)} %dynamic_slice.79, pred[4]{0:T(512)(128)(4,1)S(1)} %dynamic_slice.80), kind=kOutput, calls=%fused_computation.4.clone.1 | convolution fusion | flops 52428832 | bytes 12582933 | tf_op jit(solution)/shard_map/while/body/eval_jaxpr/rg,gic->ric/dot_general | solution.py:23
  138.2 6.6 %copy.9 = f32[4,256,1024]{2,1,0:T(8,128)} copy(f32[4,256,1024]{2,0,1:T(4,128)} %get-tuple-element.254) | data formatting | bytes 8388608 | tf_op jit(solution)/shard_map/while | solution.py:58
  147.1 10.1 %all-reduce = f32[4,256]{1,0:T(4,128)S(1)} all-reduce(f32[4,256]{1,0:T(4,128)S(1)} %fusion.33), channel_id=3, replica_groups=mesh['row'=4,'col'=8] {'row'}, use_global_device_ids=true, to_apply=%region_4.6.clone | all-reduce | flops 1024 | bytes 8192
  157.8 38.6 %reduce-scatter.3.cloned.1.call-done = f32[256,1024]{1,0:T(8,128)} async-done(((f32[1024,1024]{1,0:T(8,128)}), f32[256,1024]{1,0:T(8,128)}) %reduce-scatter.3.cloned.1.call-update) | async-done | bytes 1048592 | tf_op jit(solution)/shard_map/reduce_scatter | solution.py:60
  198.8 47.2 %all-gather.5.cloned.1.call-done = bf16[2048,1024]{1,0:T(8,128)(2,1)} async-done(((bf16[256,1024]{1,0:T(8,128)(2,1)}), bf16[2048,1024]{1,0:T(8,128)(2,1)}) %all-gather.5.cloned.1.call-update) | async-done | bytes 4194320 | tf_op jit(solution)/shard_map/all_gather | solution.py:49
  246.0 77.2 %while.29 = (s32[]{:T(128)}, f32[4,256,1024]{2,0,1:T(4,128)}, s32[16]{0:T(128)S(1)}, pred[16]{0:T(512)(128)(4,1)S(1)}, bf16[16,256,256]{2,1,0:T(8,128)(2,1)S(1)}...) while((s32[]{:T(128)}, f32[4,256,1024]{2,0,1:T(4,128)}, ...), condition=%wide.region_6.8_spmd.clone, body=%wide.region_5.7_spmd.clone.sunk | while | flops 590349312 | bytes 31986012 | solution.py:58
  246.1 2.9 gather_fusion.1
  249.0 3.8 fusion.57
  252.9 11.4 %select_add_fusion.5 = f32[4,256,1024]{2,0,1:T(4,128)} fusion(f32[4,256,1024]{2,0,1:T(4,128)} %get-tuple-element.475, f32[4,256,1024]{2,1,0:T(8,128)} %fusion.57, pred[]{:T(512)S(6)} %compare.7, s32[4]{0:T(128)S(1)} %dynamic_slice.82, pred[4]{0:T(512)(128)(4,1)S(1)} %dynamic_slice.83), kind=kOutput, calls=%fused_computation.22.clone.1 | convolution fusion | flops 52428832 | bytes 12582933 | tf_op jit(solution)/shard_map/while/body/eval_jaxpr/rg,gic->ric/dot_general | solution.py:23
  264.5 2.9 gather_fusion.1
  267.4 3.8 fusion.57
  271.3 12.7 %select_add_fusion.5 = f32[4,256,1024]{2,0,1:T(4,128)} fusion(f32[4,256,1024]{2,0,1:T(4,128)} %get-tuple-element.475, f32[4,256,1024]{2,1,0:T(8,128)} %fusion.57, pred[]{:T(512)S(6)} %compare.7, s32[4]{0:T(128)S(1)} %dynamic_slice.82, pred[4]{0:T(512)(128)(4,1)S(1)} %dynamic_slice.83), kind=kOutput, calls=%fused_computation.22.clone.1 | convolution fusion | flops 52428832 | bytes 12582933 | tf_op jit(solution)/shard_map/while/body/eval_jaxpr/rg,gic->ric/dot_general | solution.py:23
  284.1 2.9 gather_fusion.1
  287.0 3.8 fusion.57
  290.9 12.7 %select_add_fusion.5 = f32[4,256,1024]{2,0,1:T(4,128)} fusion(f32[4,256,1024]{2,0,1:T(4,128)} %get-tuple-element.475, f32[4,256,1024]{2,1,0:T(8,128)} %fusion.57, pred[]{:T(512)S(6)} %compare.7, s32[4]{0:T(128)S(1)} %dynamic_slice.82, pred[4]{0:T(512)(128)(4,1)S(1)} %dynamic_slice.83), kind=kOutput, calls=%fused_computation.22.clone.1 | convolution fusion | flops 52428832 | bytes 12582933 | tf_op jit(solution)/shard_map/while/body/eval_jaxpr/rg,gic->ric/dot_general | solution.py:23
  306.6 3.8 fusion.57
  310.5 12.7 %select_add_fusion.5 = f32[4,256,1024]{2,0,1:T(4,128)} fusion(f32[4,256,1024]{2,0,1:T(4,128)} %get-tuple-element.475, f32[4,256,1024]{2,1,0:T(8,128)} %fusion.57, pred[]{:T(512)S(6)} %compare.7, s32[4]{0:T(128)S(1)} %dynamic_slice.82, pred[4]{0:T(512)(128)(4,1)S(1)} %dynamic_slice.83), kind=kOutput, calls=%fused_computation.22.clone.1 | convolution fusion | flops 52428832 | bytes 12582933 | tf_op jit(solution)/shard_map/while/body/eval_jaxpr/rg,gic->ric/dot_general | solution.py:23
  323.2 6.6 %copy.10 = f32[4,256,1024]{2,1,0:T(8,128)} copy(f32[4,256,1024]{2,0,1:T(4,128)} %get-tuple-element.504) | data formatting | bytes 8388608 | tf_op jit(solution)/shard_map/while | solution.py:58
  329.8 51.6 %reduce-scatter.5.cloned.1.call-done = f32[256,1024]{1,0:T(8,128)} async-done(((f32[1024,1024]{1,0:T(8,128)}), f32[256,1024]{1,0:T(8,128)}) %reduce-scatter.5.cloned.1.call-update) | async-done | bytes 1048592 | tf_op jit(solution)/shard_map/reduce_scatter | solution.py:60
  (80 shorter events, 17.5 us)
Async XLA Ops:
  6.5 52.3 %all-gather.3.cloned.1.call-start = ((), (), s32[]{:S(2)}) async-start(), calls=%async_computation.2 | async-start | bytes 4718592 | tf_op jit(solution)/shard_map/all_gather | solution.py:49
  8.7 187.7 %reduce-scatter.3.cloned.1.call-start = ((), (), s32[]{:S(2)}) async-start(), calls=%async_computation.3 | async-start | bytes 5242880 | tf_op jit(solution)/shard_map/reduce_scatter | solution.py:60
  62.5 3.8 copy-start.4
  81.3 3.8 copy-start.4
  101.5 3.8 copy-start.4
  121.6 3.8 copy-start.4
  144.7 0.7 copy-start.7
  144.7 1.6 copy-start
  144.7 2.2 copy-start.5
  144.7 13.1 %copy-start.6 = (s32[256]{0:T(256)S(1)}, s32[256]{0:T(256)}, u32[]{:S(2)}) copy-start(s32[256]{0:T(256)} %param.17) | copy-start | bytes 3076
  144.7 51.7 %copy-start.2 = (f32[256,1024]{1,0:T(8,128)S(1)}, f32[256,1024]{1,0:T(8,128)}, u32[]{:S(2)}) copy-start(f32[256,1024]{1,0:T(8,128)} %param.16) | copy-start | bytes 3145732
  144.8 101.3 %copy-start.3 = (s32[16]{0:T(128)S(1)}, s32[16]{0:T(128)}, u32[]{:S(2)}) copy-start(s32[16]{0:T(128)} %get-tuple-element.525) | copy-start | bytes 196
  144.8 101.2 %all-gather.5.cloned.1.call-start = ((), (), s32[]{:S(2)}) async-start(), calls=%async_computation.4 | async-start | bytes 4718592 | tf_op jit(solution)/shard_map/all_gather | solution.py:49
  198.8 182.7 %reduce-scatter.5.cloned.1.call-start = ((), (), s32[]{:S(2)}) async-start(), calls=%async_computation.5 | async-start | bytes 5242880 | tf_op jit(solution)/shard_map/reduce_scatter | solution.py:60
  252.9 11.5 %copy-start.1 = (bf16[16,256,256]{2,1,0:T(8,128)(2,1)S(1)}, bf16[16,256,256]{2,1,0:T(8,128)(2,1)}, u32[]{:S(2)}) copy-start(bf16[16,256,256]{2,1,0:T(8,128)(2,1)} %get-tuple-element.514) | copy-start | bytes 6291460 | tf_op jit(solution)/shard_map/while
  271.3 12.7 %copy-start.1 = (bf16[16,256,256]{2,1,0:T(8,128)(2,1)S(1)}, bf16[16,256,256]{2,1,0:T(8,128)(2,1)}, u32[]{:S(2)}) copy-start(bf16[16,256,256]{2,1,0:T(8,128)(2,1)} %get-tuple-element.514) | copy-start | bytes 6291460 | tf_op jit(solution)/shard_map/while
  290.9 12.7 %copy-start.1 = (bf16[16,256,256]{2,1,0:T(8,128)(2,1)S(1)}, bf16[16,256,256]{2,1,0:T(8,128)(2,1)}, u32[]{:S(2)}) copy-start(bf16[16,256,256]{2,1,0:T(8,128)(2,1)} %get-tuple-element.514) | copy-start | bytes 6291460 | tf_op jit(solution)/shard_map/while
  310.5 12.7 %copy-start.1 = (bf16[16,256,256]{2,1,0:T(8,128)(2,1)S(1)}, bf16[16,256,256]{2,1,0:T(8,128)(2,1)}, u32[]{:S(2)}) copy-start(bf16[16,256,256]{2,1,0:T(8,128)(2,1)} %get-tuple-element.514) | copy-start | bytes 6291460 | tf_op jit(solution)/shard_map/while
Sparse Core Ops, SparseCore 0:
  9.0 49.8 all-gather.2
  144.9 51.4 reduce-scatter.2
  198.9 47.1 all-gather.4
  330.0 51.4 reduce-scatter.4
where the time goes:
time: 391 us; the launch traced here: 390 us
  waiting for transfers between devices  187 us (48%)
  matrix products  129 us (33%)
  local copies, waits for them, and re-layouts  39.3 us (10%)
  between operations  13.9 us (4%)
  other arithmetic  10.9 us (3%)
  blocking collectives  10.1 us (3%)
    dot_general x8, matrix products, group_term(): jnp.einsum('rg,gic->ric', placing, product, precision=lax.Precision.HIGHEST)  98.6 us
    all_gather x2, waiting for transfers between devices, on_device(): lax.all_gather(current.astype(jnp.bfloat16), 'col', axis=0, tiled=True)  96.7 us
    reduce_scatter x2, waiting for transfers between devices, on_device(): lax.psum_scatter(flat_terms, 'row', scatter_dimension=0, tiled=True)  90.2 us
    dot_general x8, matrix products, group_term(): jnp.einsum('gij,gjc->gic', tile_group, fetched, preferred_element_type=jn...  30.3 us
    gather x8, local copies, waits for them, and re-layouts, group_term(): fetched = jnp.take(gathered, group_cols, axis=0)  23 us
    while x2, local copies, waits for them, and re-layouts, on_device(): running = lax.fori_loop(0, group_total, add_group, empty)  13.1 us
    unnamed x1, blocking collectives  10.1 us
  transfers between devices with their start and end apart: 4, of which 4 were waited for; matrix products, arithmetic and copies ran while one was open for 1% of the time, Pallas kernels for 0%

commit v1 on v0

v1 whole, which is shorter than its diff:
```python
import functools

import jax
import jax.numpy as jnp
from jax import lax
from jax.experimental import pallas as pl
from jax.experimental.pallas import tpu as pltpu
from jax.sharding import PartitionSpec as P

SWEEPS = 2
PARTS = [2, 1, 1]
FORWARD = 0
SMALL = 1
ORDER = ("A0", "A1", "D0", "A2", "D1", "U0", "D2", "U1", "D3", "U2", "D4", "D5", "U3", "U4", "U5")
DENSE_LIMIT = 14
TERM_LIMIT = 14
UPDATE_LIMIT = 4
spread_weight = 0.8

COST = None
FREE = pl.CostEstimate(flops=0, bytes_accessed=0, transcendentals=0)
MIB = 1024 * 1024
LANES = 128
PIN = 1


def dense_kernel(slot_ref, tiles_ref, near_tiles_ref, dense_ref, degree_ref, column_ref):
    rows_n = slot_ref.shape[0]
    side = tiles_ref.shape[1]
    places = dense_ref.shape[1] // side
    ones = jnp.ones((8, dense_ref.shape[1]), dense_ref.dtype)
    ones_down = jnp.ones((dense_ref.shape[1], LANES), dense_ref.dtype)

    def line(i, _):
        for e, source in enumerate((tiles_ref, near_tiles_ref)):
            at = pl.ds(pl.multiple_of((e * rows_n + i) * side, side), side)
            for q in range(places):
                slot = slot_ref[i, e * places + q]
                tile = source[jnp.maximum(slot, 0)]
                dense_ref[at, q * side : (q + 1) * side] = jnp.where(slot >= 0, tile, jnp.zeros_like(tile))
            degree_ref[pl.ds(pl.multiple_of((e * rows_n + i) * 8, 8), 8)] = lax.dot_general(
                ones, dense_ref[at], (((1,), (1,)), ((), ())), preferred_element_type=jnp.float32
            )
            column_ref[at] = jnp.dot(dense_ref[at], ones_down, preferred_element_type=jnp.float32)
        return 0

    lax.fori_loop(0, rows_n, line, 0)


def dense_tiles(table, tiles, near_tiles):
    rows_n, places = table.shape
    side = tiles.shape[1]
    dense = jax.ShapeDtypeStruct((2 * rows_n * side, places // 2 * side), tiles.dtype)
    if PIN and dense.size * 2 <= 8 * MIB:
        dense = pltpu.VMEM(dense.shape, dense.dtype)
    return pl.pallas_call(
        dense_kernel,
        out_shape=[
            dense,
            jax.ShapeDtypeStruct((2 * rows_n * 8, side), jnp.float32),
            jax.ShapeDtypeStruct((2 * rows_n * side, LANES), jnp.float32),
        ],
        in_specs=[pl.BlockSpec(memory_space=pltpu.SMEM)] + [pl.BlockSpec(memory_space=pltpu.VMEM)] * 2,
        out_specs=[pl.BlockSpec(memory_space=pltpu.VMEM)] * 3,
        compiler_params=pltpu.CompilerParams(vmem_limit_bytes=(DENSE_LIMIT if dense.shape[0] * dense.shape[1] <= 4 * MIB else 56) * MIB),
        cost_estimate=FREE,
    )(table, tiles, near_tiles)


def term_kernel(count, rows_n, extra, token_ref, dense_ref, *refs):
    block_refs, extra_refs = refs[:count], refs[count : count + extra]
    next_ref, *term_refs = refs[count + extra :]
    next_ref[...] = token_ref[...]
    blocks = [r[...] for r in block_refs]
    if count == 5:
        blocks = blocks[:3] + [blocks[3] + blocks[4]]
    depth = blocks[0].shape[0]
    side = depth // 2
    for e in range(2):
        lines = slice(e * rows_n * side, (e + 1) * rows_n * side)
        total = None
        for k, block in enumerate(blocks):
            product = jnp.dot(
                dense_ref[lines, k * depth : (k + 1) * depth], block, preferred_element_type=jnp.float32
            )
            total = product if total is None else total + product
        for m, term_ref in enumerate(term_refs):
            term_ref[e * side : (e + 1) * side] = total[m * side : (m + 1) * side]
    for extra_ref, term_ref in zip(extra_refs, term_refs):
        term_ref[depth:] = extra_ref[...]


def term_step_kernel(count, rows_n, extra, token_ref, dense_ref, *refs):
    block_refs, extra_refs = refs[:count], refs[count : count + extra]
    next_ref, *term_refs = refs[count + extra :]
    next_ref[...] = token_ref[...]
    depth = block_refs[0].shape[0]
    side = depth // 2
    e, line = pl.program_id(0), pl.program_id(1)
    total = None
    for k, block_ref in enumerate(block_refs):
        product = jnp.dot(
            dense_ref[:, k * depth : (k + 1) * depth], block_ref[...], preferred_element_type=jnp.float32
        )
        total = product if total is None else total + product
    for m, term_ref in enumerate(term_refs):

        @pl.when(line == m)
        def _():
            term_ref[pl.ds(pl.multiple_of(e * side, side), side)] = total
            if extra:
                term_ref[depth:] = extra_refs[m][...]


def terms(token, dense, blocks, extras, rows_n):
    side = dense.shape[0] // (2 * rows_n)
    width = blocks[0].shape[1]
    rows = 2 * side + (extras[0].shape[0] if extras else 0)
    whole = dense.size * 2 <= 8 * MIB
    vmem = pl.BlockSpec(memory_space=pltpu.VMEM)
    others = len(blocks) + len(extras)
    if whole:
        dense = pltpu.with_memory_space_constraint(dense, pltpu.VMEM) if PIN else dense
        split = dict(in_specs=[vmem] * (2 + others), out_specs=[vmem] * (1 + rows_n))
    else:
        at_start = lambda x: pl.BlockSpec(x.shape, lambda e, m: (0, 0))
        out = jax.ShapeDtypeStruct((rows, width), jnp.float32)
        split = dict(
            grid=(2, rows_n),
            in_specs=[at_start(token), pl.BlockSpec((side, dense.shape[1]), lambda e, m: (e * rows_n + m, 0))]
            + [at_start(x) for x in (*blocks, *extras)],
            out_specs=[at_start(token)] + [at_start(out)] * rows_n,
        )
    token, *out = pl.pallas_call(
        functools.partial(term_kernel if whole else term_step_kernel, len(blocks), rows_n, len(extras)),
        out_shape=[jax.ShapeDtypeStruct(token.shape, token.dtype)]
        + [jax.ShapeDtypeStruct((rows, width), jnp.float32)] * rows_n,
        compiler_params=pltpu.CompilerParams(vmem_limit_bytes=(TERM_LIMIT if whole else 48) * MIB),
        cost_estimate=None if COST is None else pl.CostEstimate(flops=int(COST * 1e9 * width / 512), bytes_accessed=0, transcendentals=0),
        **split,
    )(token, dense, *blocks, *extras)
    return token, out


def begin_kernel(token_ref, kept_ref, got_ref, next_ref, prior_ref, coarse_ref):
    side = kept_ref.shape[0]
    next_ref[...] = token_ref[...]
    for k, ref in enumerate((kept_ref, got_ref)):
        prior_ref[k * side : (k + 1) * side] = ref[...]
        coarse_ref[k * side : (k + 1) * side] = ref[...].astype(jnp.bfloat16)


def begin(token, kept, got):
    rows, width = 2 * kept.shape[0], kept.shape[1]
    vmem = pl.BlockSpec(memory_space=pltpu.VMEM)
    return pl.pallas_call(
        begin_kernel,
        out_shape=[
            jax.ShapeDtypeStruct(token.shape, token.dtype),
            jax.ShapeDtypeStruct((rows, width), jnp.float32),
            jax.ShapeDtypeStruct((rows, width), jnp.bfloat16),
        ],
        in_specs=[vmem] * 3,
        out_specs=[vmem] * 3,
        compiler_params=pltpu.CompilerParams(vmem_limit_bytes=UPDATE_LIMIT * MIB),
        cost_estimate=FREE,
    )(token, kept, got)


def update_kernel(token_ref, keep_ref, scale_ref, prior_ref, own_ref, *refs):
    *got_refs, next_ref, out_ref = refs
    next_ref[...] = token_ref[...]
    spread(keep_ref, scale_ref, prior_ref, own_ref, got_refs, out_ref)


def spread(keep_ref, scale_ref, prior_ref, own_ref, got_refs, out_ref):
    rows, width = out_ref.shape
    for at in range(0, width, LANES):
        lanes = slice(at, at + LANES)
        summed = own_ref[:rows, lanes]
        for got_ref in got_refs:
            summed += got_ref[:rows, lanes]
        prior = prior_ref[:, lanes]
        value = scale_ref[...] * summed + (1.0 - spread_weight) * prior
        out_ref[:, lanes] = jnp.where(keep_ref[...] > 0, prior, value).astype(out_ref.dtype)


def first_update_kernel(count, token_ref, labelled_ref, prior_ref, *refs):
    term_refs, (next_ref, out_ref, keep_ref, scale_ref, *column_refs) = refs[:count], refs[count:]
    next_ref[...] = token_ref[...]
    rows, width = out_ref.shape

    def turn(ref, first):
        for at in range(0, rows, LANES):
            line, lane = first + at // ref.shape[1], at % ref.shape[1]
            flat = jnp.broadcast_to(ref[line : line + 1, lane : lane + LANES], (LANES, LANES))
            yield slice(at, at + LANES), flat.T

    for at, column in turn(labelled_ref, 0):
        keep_ref[at] = column
    for term_ref, column_ref in zip(term_refs, column_refs):
        for at, column in turn(term_ref, rows):
            column_ref[at] = column
    total = column_refs[0][...]
    for column_ref in column_refs[1:]:
        total += column_ref[...]
    scale_ref[...] = spread_weight / total
    spread(keep_ref, scale_ref, prior_ref, term_refs[0], term_refs[1:], out_ref)


def update(token, keep, scale, prior, own, got):
    vmem = pl.BlockSpec(memory_space=pltpu.VMEM)
    return pl.pallas_call(
        update_kernel,
        out_shape=[
            jax.ShapeDtypeStruct(token.shape, token.dtype),
            jax.ShapeDtypeStruct(prior.shape, jnp.bfloat16),
        ],
        in_specs=[vmem] * (5 + len(got)),
        out_specs=[vmem] * 2,
        compiler_params=pltpu.CompilerParams(vmem_limit_bytes=UPDATE_LIMIT * MIB),
        cost_estimate=FREE,
    )(token, keep, scale, prior, own, *got)


def first_update(token, labelled, prior, terms_in):
    vmem = pl.BlockSpec(memory_space=pltpu.VMEM)
    column = jax.ShapeDtypeStruct((prior.shape[0], LANES), jnp.float32)
    return pl.pallas_call(
        functools.partial(first_update_kernel, len(terms_in)),
        out_shape=[
            jax.ShapeDtypeStruct(token.shape, token.dtype),
            jax.ShapeDtypeStruct(prior.shape, jnp.bfloat16),
        ]
        + [column] * (2 + len(terms_in)),
        in_specs=[vmem] * (3 + len(terms_in)),
        out_specs=[vmem] * (4 + len(terms_in)),
        compiler_params=pltpu.CompilerParams(vmem_limit_bytes=2 * UPDATE_LIMIT * MIB),
        cost_estimate=FREE,
    )(token, labelled, prior, *terms_in)


def swap(x, axis, mask):
    size = lax.axis_size(axis)
    return lax.ppermute(x, axis, [(i, i ^ mask) for i in range(size)])


def on_device(affinity, block_rows, block_cols, block_count, labels, labelled):
    tiles = affinity[0, 0]
    rows_n = lax.axis_size("row")
    cols_n = lax.axis_size("col")
    slots, side, _ = tiles.shape
    half = labels.shape[1] // 2
    row, col = lax.axis_index("row"), lax.axis_index("col")
    core = col & 1

    count = len(PARTS)
    widths = [half * p // sum(PARTS) for p in PARTS]
    starts = [sum(widths[:i]) for i in range(count)]
    halves = []
    for s, w in zip(starts, widths):
        kept = lax.dynamic_slice_in_dim(labels, core * half + s, w, 1)
        given = lax.dynamic_slice_in_dim(labels, (1 - core) * half + s, w, 1)
        halves.append((kept, swap(given, "col", 1)))

    live = jnp.arange(slots) < block_count[0, 0]
    hit = (
        ((block_rows[0, 0] ^ row)[None, None, :] == jnp.arange(rows_n)[:, None, None])
        & ((block_cols[0, 0] ^ col)[None, None, :] == jnp.arange(cols_n)[None, :, None])
        & live[None, None, :]
    )
    table = jnp.max(jnp.where(hit, jnp.arange(slots), -1), axis=2).astype(jnp.int32)
    near_tiles = swap(tiles, "col", 1)
    numbers = jnp.concatenate([table.reshape(-1), labelled])
    near_numbers = swap(numbers, "col", 1)
    near_table = near_numbers[: rows_n * cols_n].reshape(rows_n, cols_n // 2, 2)
    near_table = near_table[:, :, ::-1].reshape(rows_n, cols_n)
    table = jnp.concatenate([table, near_table], axis=1)
    both = jnp.concatenate([labelled, near_numbers[rows_n * cols_n :]])
    both = jnp.pad((both == 1).astype(jnp.float32).reshape(-1, LANES), ((0, -(2 * side // LANES) % 8), (0, 0)))
    inner = [i for i in range(cols_n) if (i >> 1) & 3 in (1, 2)]

    dense, part, columns = dense_tiles(table, tiles, near_tiles)
    part = part.reshape(2, rows_n, 8, side)[:, :, 0]
    part = [part[:, m].reshape(2 * side) for m in range(rows_n)]
    columns = columns.reshape(2, rows_n, side, LANES)
    columns = [columns[:, m].reshape(2 * side, LANES) for m in range(rows_n)]

    def wide(x, width):
        return jnp.concatenate([x] * (width // LANES), axis=1)

    token = start = jnp.zeros((8, 128), jnp.float32)
    priors, held, sums, final = {}, {}, {}, {}
    degrees = None

    def spread_out(x):
        if FORWARD:
            far = swap(x, "col", 4)
            blocks = [
                x,
                swap(x, "col", 2),
                far,
                lax.ppermute(x, "col", [(i, i ^ 6) for i in inner]),
                lax.ppermute(far, "col", [(i, i ^ 2) for i in inner]),
            ]
            if cols_n > 8:
                blocks = blocks[:3] + [blocks[3] + blocks[4]]
        else:
            blocks = [x] + [swap(x, "col", 2 * k) for k in range(1, min(4, cols_n // 2))]
        while 4 <= len(blocks) < cols_n // 2:
            blocks = blocks + [swap(b, "col", 2 * len(blocks)) for b in blocks]
        return blocks

    for name in ORDER:
        kind, n = name[0], int(name[1:])
        c, last = n % count, n >= count * (SWEEPS - 1)
        width = widths[c]
        free, token = token, (start if kind.islower() else token)
        kind = kind.upper()
        if kind == "A":
            token, priors[c], coarse = begin(token, *halves[c])
            held[n] = spread_out(coarse)
        elif kind == "D":
            extras = []
            if degrees is None:
                lines = 2 * side // width
                extras = [jnp.pad(p.reshape(lines, width), ((0, -lines % 8), (0, 0))) for p in part]
                degrees = n
            token, term = terms(token, dense, held.pop(n), extras, rows_n)
            if last and SMALL:
                sent = [(t / wide(p, width)).astype(jnp.float16) for t, p in zip(term[1:], columns[1:])]
            else:
                sent = term[1:]
            sums[n] = [term[0]] + [swap(x, "row", m + 1) for m, x in enumerate(sent)]
        elif not last:
            if n == degrees:
                token, coarse, keep, scale, *degrees = first_update(token, both, priors[c], sums.pop(n))
            else:
                own, *got = sums.pop(n)
                token, coarse = update(token, keep, scale, priors[c], own, got)
            held[n + count] = spread_out(coarse)
        else:
            own, *got = sums.pop(n)
            if SMALL:
                got = [x.astype(jnp.float32) * wide(p, width) for x, p in zip(got, degrees[1:])]
            prior = priors[c]
            out = jnp.where(
                wide(keep, width) > 0,
                prior,
                wide(scale, width) * (own + sum(got)) + (1.0 - spread_weight) * prior,
            )
            final[c] = out[:side], swap(out[side:], "col", 1)
        if name[0].islower():
            token = free
    final = [final[c] for c in range(count)]
    mine, other = (jnp.concatenate([f[k] for f in final], axis=1) for k in (0, 1))
    low, high = jnp.where(core == 0, mine, other), jnp.where(core == 0, other, mine)
    return jnp.concatenate([low, high], axis=1)


def solution(mesh):
    placed = (
        P("row", "col", None, None, None),
        P("row", "col", None),
        P("row", "col", None),
        P("row", "col"),
        P(("row", "col"), None),
        P(("row", "col")),
    )
    return jax.shard_map(
        on_device, mesh=mesh, in_specs=placed, out_specs=P(("row", "col"), None), check_vma=False
    )
```

time: 391 us -> 143 us (0.37)
  waiting for transfers between devices: 187 us -> 38.4 us
  matrix products: 129 us -> 0 us
  starting transfers between devices: 0.31 us -> 58.8 us
  Pallas kernels: 0 us -> 25.7 us
  local copies, waits for them, and re-layouts: 39.3 us -> 15.3 us
  between operations: 13.9 us -> 1.08 us
  blocking collectives: 10.1 us -> 0 us
  other arithmetic: 10.9 us -> 2.76 us
    dot_general x17 -> x0, matrix products: 129 us -> none  [the longest x8 98.6 us: group_term(): jnp.einsum('rg,gic->ric', placing, product, precision=lax.Precision.HIGHEST)]
    all_gather x2 -> x0, waiting for transfers between devices: 96.7 us -> none  [on_device(): lax.all_gather(current.astype(jnp.bfloat16), 'col', axis=0, tiled=True)]
    reduce_scatter x2 -> x0, waiting for transfers between devices: 90.2 us -> none  [on_device(): lax.psum_scatter(flat_terms, 'row', scatter_dimension=0, tiled=True)]
    ppermute x0 -> x44, starting transfers between devices: none -> 58.8 us  [swap(): return lax.ppermute(x, axis, [(i, i ^ mask) for i in range(size)])]
    ppermute x0 -> x44, waiting for transfers between devices: none -> 38.4 us  [swap(): return lax.ppermute(x, axis, [(i, i ^ mask) for i in range(size)])]
    pallas_call x0 -> x13, Pallas kernels: none -> 25.7 us  [the longest x6 16.3 us: terms(): pl.pallas_call(functools.partial(term_kernel if whole else term_step_kern...]
    gather x8 -> x0, local copies, waits for them, and re-layouts: 23 us -> none  [group_term(): fetched = jnp.take(gathered, group_cols, axis=0)]
    while x18 -> x0, local copies, waits for them, and re-layouts: 13.2 us -> none  [the longest x2 13.1 us: on_device(): running = lax.fori_loop(0, group_total, add_group, empty)]
  transfers between devices with their start and end apart: 4 -> 44, of which waited for: 4 -> 17; matrix products, arithmetic and copies ran while one was open for 1% -> 3% of each run, Pallas kernels for 0% -> 18%
where the time goes in v1:
time: 143 us; the launch traced here: 142 us
  starting transfers between devices  58.8 us (41%)
  waiting for transfers between devices  38.4 us (27%)
  Pallas kernels  25.7 us (18%)
  local copies, waits for them, and re-layouts  15.3 us (11%)
  other arithmetic  2.76 us (2%)
    ppermute x44, starting transfers between devices, swap(): return lax.ppermute(x, axis, [(i, i ^ mask) for i in range(size)])  58.8 us
    ppermute x44, waiting for transfers between devices, swap(): return lax.ppermute(x, axis, [(i, i ^ mask) for i in range(size)])  38.4 us
    pallas_call x6, Pallas kernels, terms(): pl.pallas_call(functools.partial(term_kernel if whole else term_step_kern...  16.3 us
    unnamed x39, local copies, waits for them, and re-layouts  12.4 us
    pallas_call x1, Pallas kernels, dense_tiles(): pl.pallas_call(dense_kernel, out_shape=[dense, jax.ShapeDtypeStruct((2 *...  6.65 us
  transfers between devices with their start and end apart: 44, of which 17 were waited for; matrix products, arithmetic and copies ran while one was open for 3% of the time, Pallas kernels for 18%

profile of v1, /device:TPU:0, one launch (start us, length us, event | category | flops | bytes accessed | tf_op | source)
XLA Modules:
  0.0 142.1 jit_solution(597723466702894156)
XLA Ops:
  6.1 2.8 %collective-permute-start.4 = (bf16[512,256]{1,0:T(8,128)(2,1)S(1)}, bf16[512,256]{1,0:T(8,128)(2,1)S(1)}, u32[]{:S(2)}, u32[]{:S(2)}) collective-permute-start(bf16[512,256]{1,0:T(8,128)(2,1)S(1)} %get-tuple-element.60.refs_0_), channel_id=1, source_target_pairs={{0,2},{1,3},{2,0},{3,1},{4,6},{5,7},{6,4},{7,5},{8,10},{9,11},{10,... | collective-permute-start | bytes 786440 | tf_op jit(solution)/shard_map/ppermute | solution.py:245
  8.9 2.6 %collective-permute-start.5 = (bf16[512,256]{1,0:T(8,128)(2,1)S(1)}, bf16[512,256]{1,0:T(8,128)(2,1)S(1)}, u32[]{:S(2)}, u32[]{:S(2)}) collective-permute-start(bf16[512,256]{1,0:T(8,128)(2,1)S(1)} %get-tuple-element.60.refs_0_), channel_id=1, source_target_pairs={{0,4},{1,5},{2,6},{3,7},{4,0},{5,1},{6,2},{7,3},{8,12},{9,13},{10,... | collective-permute-start | bytes 786440 | tf_op jit(solution)/shard_map/ppermute | solution.py:245
  11.6 1.6 %copy-done.2 = bf16[1,1,16,256,256]{4,3,2,1,0:T(8,128)(2,1)S(1)} copy-done((bf16[1,1,16,256,256]{4,3,2,1,0:T(8,128)(2,1)S(1)}, bf16[1,1,16,256,256]{4,3,2,1,0:T(8,128)(2,1)}, u32[]{:S(2)}) %copy-start.2) | copy-done | bytes 2097176
  13.2 6.6 %shard_map.66 = (bf16[2048,2048]{1,0:T(8,128)(2,1)S(1)}, f32[64,256]{1,0:T(8,128)S(1)}, f32[2048,128]{1,0:T(8,128)S(1)}) custom-call(s32[4,16]{1,0:T(4,128)S(1)} %pad_add_fusion.1.slot_ref, bf16[16,256,256]{2,1,0:T(8,128)(2,1)S(1)} %bitcast.40, bf16[16,256,256]{2,1,0:T(8,128)(2,1)} %collective-permute-done.3.near_tiles_ref), custom_call_target="tpu_custom_call" | custom-call | tf_op jit(solution)/shard_map/pallas_call | solution.py:56
  20.8 9.4 %collective-permute-done.5.refs_2_ = bf16[512,256]{1,0:T(8,128)(2,1)S(1)} collective-permute-done((bf16[512,256]{1,0:T(8,128)(2,1)S(1)}, bf16[512,256]{1,0:T(8,128)(2,1)S(1)}, u32[]{:S(2)}, u32[]{:S(2)}) %collective-permute-start.5) | collective-permute-done | bytes 262176 | tf_op jit(solution)/shard_map/ppermute | solution.py:245
  30.2 2.3 %shard_map.67 = (f32[8,128]{1,0:T(8,128)S(1)}, f32[520,256]{1,0:T(8,128)S(1)}, f32[520,256]{1,0:T(8,128)S(1)}, f32[520,256]{1,0:T(8,128)S(1)}, f32[520,256]{1,0:T(8,128)S(1)}) custom-call(f32[8,128]{1,0:T(8,128)S(1)} %get-tuple-element.58.token_ref, bf16[2048,2048]{1,0:T(8,128)(2,1)S(1)} %get-tuple-element.59.dense_ref, ...), custom_call_target="tpu_custom_call" | custom-call | tf_op jit(solution)/shard_map/pallas_call | solution.py:134
  32.5 1.6 %collective-permute-start.11 = (f32[520,256]{1,0:T(8,128)S(1)}, f32[520,256]{1,0:T(8,128)S(1)}, u32[]{:S(2)}, u32[]{:S(2)}) collective-permute-start(f32[520,256]{1,0:T(8,128)S(1)} %get-tuple-element.68), channel_id=1, source_target_pairs={{0,8},{8,0},{16,24},{24,16},{1,9},{9,1},{17,25},{25,17},{2,10},{10... | collective-permute-start | bytes 1597448 | tf_op jit(solution)/shard_map/ppermute | solution.py:245
  36.1 5.3 %collective-permute-start.8 = (bf16[512,128]{1,0:T(8,128)(2,1)S(1)}, bf16[512,128]{1,0:T(8,128)(2,1)S(1)}, u32[]{:S(2)}, u32[]{:S(2)}) collective-permute-start(bf16[512,128]{1,0:T(8,128)(2,1)S(1)} %get-tuple-element.64.refs_0_), channel_id=1, source_target_pairs={{0,2},{1,3},{2,0},{3,1},{4,6},{5,7},{6,4},{7,5},{8,10},{9,11},{10,... | collective-permute-start | bytes 393224 | tf_op jit(solution)/shard_map/ppermute | solution.py:245
  42.5 3.1 %collective-permute-done.8.refs_1_ = bf16[512,128]{1,0:T(8,128)(2,1)S(1)} collective-permute-done((bf16[512,128]{1,0:T(8,128)(2,1)S(1)}, bf16[512,128]{1,0:T(8,128)(2,1)S(1)}, u32[]{:S(2)}, u32[]{:S(2)}) %collective-permute-start.8) | collective-permute-done | bytes 131104 | tf_op jit(solution)/shard_map/ppermute | solution.py:245
  47.1 4.5 %collective-permute-done.9.refs_2_ = bf16[512,128]{1,0:T(8,128)(2,1)S(1)} collective-permute-done((bf16[512,128]{1,0:T(8,128)(2,1)S(1)}, bf16[512,128]{1,0:T(8,128)(2,1)S(1)}, u32[]{:S(2)}, u32[]{:S(2)}) %collective-permute-start.9) | collective-permute-done | bytes 131104 | tf_op jit(solution)/shard_map/ppermute | solution.py:245
  52.8 3.1 %collective-permute-start.15 = (bf16[512,128]{1,0:T(8,128)(2,1)S(1)}, bf16[512,128]{1,0:T(8,128)(2,1)S(1)}, u32[]{:S(2)}, u32[]{:S(2)}) collective-permute-start(bf16[512,128]{1,0:T(8,128)(2,1)S(1)} %get-tuple-element.74.refs_0_), channel_id=1, source_target_pairs={{0,4},{1,5},{2,6},{3,7},{4,0},{5,1},{6,2},{7,3},{8,12},{9,13},{10,... | collective-permute-start | bytes 393224 | tf_op jit(solution)/shard_map/ppermute | solution.py:245
  55.9 2.3 %shard_map.69 = (f32[8,128]{1,0:T(8,128)S(1)}, f32[512,128]{1,0:T(8,128)S(1)}, f32[512,128]{1,0:T(8,128)S(1)}, f32[512,128]{1,0:T(8,128)S(1)}, f32[512,128]{1,0:T(8,128)S(1)}) custom-call(f32[8,128]{1,0:T(8,128)S(1)} %get-tuple-element.63.token_ref, bf16[2048,2048]{1,0:T(8,128)(2,1)S(1)} %get-tuple-element.59.dense_ref, ...), custom_call_target="tpu_custom_call" | custom-call | tf_op jit(solution)/shard_map/pallas_call | solution.py:134
  58.3 1.6 %collective-permute-start.17 = (f32[512,128]{1,0:T(8,128)S(1)}, f32[512,128]{1,0:T(8,128)S(1)}, u32[]{:S(2)}, u32[]{:S(2)}) collective-permute-start(f32[512,128]{1,0:T(8,128)S(1)} %get-tuple-element.78), channel_id=1, source_target_pairs={{0,8},{8,0},{16,24},{24,16},{1,9},{9,1},{17,25},{25,17},{2,10},{10... | collective-permute-start | bytes 786440 | tf_op jit(solution)/shard_map/ppermute | solution.py:245
  63.1 4.9 %collective-permute-start.20 = (bf16[512,256]{1,0:T(8,128)(2,1)}, bf16[512,256]{1,0:T(8,128)(2,1)S(1)}, u32[]{:S(2)}, u32[]{:S(2)}) collective-permute-start(bf16[512,256]{1,0:T(8,128)(2,1)} %get-tuple-element.82.refs_0_), channel_id=1, source_target_pairs={{0,2},{1,3},{2,0},{3,1},{4,6},{5,7},{6,4},{7,5},{8,10},{9,11},{10,... | collective-permute-start | bytes 786440 | tf_op jit(solution)/shard_map/ppermute | solution.py:245
  68.1 2.5 %collective-permute-start.16 = (bf16[512,128]{1,0:T(8,128)(2,1)S(1)}, bf16[512,128]{1,0:T(8,128)(2,1)S(1)}, u32[]{:S(2)}, u32[]{:S(2)}) collective-permute-start(bf16[512,128]{1,0:T(8,128)(2,1)S(1)} %get-tuple-element.74.refs_0_), channel_id=1, source_target_pairs={{0,6},{1,7},{2,4},{3,5},{4,2},{5,3},{6,0},{7,1},{8,14},{9,15},{10,... | collective-permute-start | bytes 393224 | tf_op jit(solution)/shard_map/ppermute | solution.py:245
  70.6 8.4 %collective-permute-done.16.refs_3_ = bf16[512,128]{1,0:T(8,128)(2,1)S(1)} collective-permute-done((bf16[512,128]{1,0:T(8,128)(2,1)S(1)}, bf16[512,128]{1,0:T(8,128)(2,1)S(1)}, u32[]{:S(2)}, u32[]{:S(2)}) %collective-permute-start.16) | collective-permute-done | bytes 131104 | tf_op jit(solution)/shard_map/ppermute | solution.py:245
  79.0 3.1 %shard_map.71 = (f32[8,128]{1,0:T(8,128)S(1)}, f32[512,128]{1,0:T(8,128)S(1)}, f32[512,128]{1,0:T(8,128)}, f32[512,128]{1,0:T(8,128)}, f32[512,128]{1,0:T(8,128)}) custom-call(f32[8,128]{1,0:T(8,128)S(1)} %get-tuple-element.73.token_ref, bf16[2048,2048]{1,0:T(8,128)(2,1)S(1)} %get-tuple-element.59.dense_ref, bf16[512,128]{1,0:T(8,128)(2,1)S(1)} %get-tuple-element.74.refs_0_, ...), custom_call_target="tpu_custom_call" | custom-call | tf_op jit(solution)/shard_map/pallas_call | solution.py:134
  84.4 1.6 %collective-permute-start.26 = (f32[512,128]{1,0:T(8,128)}, f32[512,128]{1,0:T(8,128)}, u32[]{:S(2)}, u32[]{:S(2)}) collective-permute-start(f32[512,128]{1,0:T(8,128)} %get-tuple-element.94), channel_id=1, source_target_pairs={{0,8},{8,0},{16,24},{24,16},{1,9},{9,1},{17,25},{25,17},{2,10},{10... | collective-permute-start | bytes 786440 | tf_op jit(solution)/shard_map/ppermute | solution.py:245
  86.7 2.5 %collective-permute-start.27 = (f32[512,128]{1,0:T(8,128)}, f32[512,128]{1,0:T(8,128)}, u32[]{:S(2)}, u32[]{:S(2)}) collective-permute-start(f32[512,128]{1,0:T(8,128)} %get-tuple-element.95), channel_id=1, source_target_pairs={{0,16},{8,24},{16,0},{24,8},{1,17},{9,25},{17,1},{25,9},{2,18},{10... | collective-permute-start | bytes 786440 | tf_op jit(solution)/shard_map/ppermute | solution.py:245
  95.1 1.6 %collective-permute-start.29 = (bf16[512,128]{1,0:T(8,128)(2,1)S(1)}, bf16[512,128]{1,0:T(8,128)(2,1)S(1)}, u32[]{:S(2)}, u32[]{:S(2)}) collective-permute-start(bf16[512,128]{1,0:T(8,128)(2,1)S(1)} %get-tuple-element.98.refs_0_), channel_id=1, source_target_pairs={{0,2},{1,3},{2,0},{3,1},{4,6},{5,7},{6,4},{7,5},{8,10},{9,11},{10,... | collective-permute-start | bytes 393224 | tf_op jit(solution)/shard_map/ppermute | solution.py:245
  96.7 2.8 %collective-permute-start.30 = (bf16[512,128]{1,0:T(8,128)(2,1)S(1)}, bf16[512,128]{1,0:T(8,128)(2,1)S(1)}, u32[]{:S(2)}, u32[]{:S(2)}) collective-permute-start(bf16[512,128]{1,0:T(8,128)(2,1)S(1)} %get-tuple-element.98.refs_0_), channel_id=1, source_target_pairs={{0,4},{1,5},{2,6},{3,7},{4,0},{5,1},{6,2},{7,3},{8,12},{9,13},{10,... | collective-permute-start | bytes 393224 | tf_op jit(solution)/shard_map/ppermute | solution.py:245
  99.5 3.4 %copy-done.1 = bf16[2048,2048]{1,0:T(8,128)(2,1)S(1)} copy-done((bf16[2048,2048]{1,0:T(8,128)(2,1)S(1)}, bf16[2048,2048]{1,0:T(8,128)(2,1)}, u32[]{:S(2)}) %copy-start.1) | copy-done | bytes 8388632
  102.9 3.5 %shard_map.73 = (f32[8,128]{1,0:T(8,128)S(1)}, f32[512,256]{1,0:T(8,128)S(1)}, f32[512,256]{1,0:T(8,128)S(1)}, f32[512,256]{1,0:T(8,128)S(1)}, f32[512,256]{1,0:T(8,128)S(1)}) custom-call(f32[8,128]{1,0:T(8,128)S(1)} %get-tuple-element.81.token_ref, bf16[2048,2048]{1,0:T(8,128)(2,1)S(1)} %copy-done.1, bf16[512,256]{1,0:T(8,128)(2,1)} %get-tuple-element.82.refs_0_, ...), custom_call_target="tpu_custom_call" | custom-call | tf_op jit(solution)/shard_map/pallas_call | solution.py:134
  106.4 2.2 %collective-permute-start.31 = (bf16[512,128]{1,0:T(8,128)(2,1)S(1)}, bf16[512,128]{1,0:T(8,128)(2,1)S(1)}, u32[]{:S(2)}, u32[]{:S(2)}) collective-permute-start(bf16[512,128]{1,0:T(8,128)(2,1)S(1)} %get-tuple-element.98.refs_0_), channel_id=1, source_target_pairs={{0,6},{1,7},{2,4},{3,5},{4,2},{5,3},{6,0},{7,1},{8,14},{9,15},{10,... | collective-permute-start | bytes 393224 | tf_op jit(solution)/shard_map/ppermute | solution.py:245
  109.9 2.2 %collective-permute-start.36 = (bf16[512,128]{1,0:T(8,128)(2,1)S(1)}, bf16[512,128]{1,0:T(8,128)(2,1)S(1)}, u32[]{:S(2)}, u32[]{:S(2)}) collective-permute-start(bf16[512,128]{1,0:T(8,128)(2,1)S(1)} %get-tuple-element.104.refs_0_), channel_id=1, source_target_pairs={{0,4},{1,5},{2,6},{3,7},{4,0},{5,1},{6,2},{7,3},{8,12},{9,13},{10,... | collective-permute-start | bytes 393224 | tf_op jit(solution)/shard_map/ppermute | solution.py:245
  112.3 2.2 %collective-permute-start.37 = (bf16[512,128]{1,0:T(8,128)(2,1)S(1)}, bf16[512,128]{1,0:T(8,128)(2,1)S(1)}, u32[]{:S(2)}, u32[]{:S(2)}) collective-permute-start(bf16[512,128]{1,0:T(8,128)(2,1)S(1)} %get-tuple-element.104.refs_0_), channel_id=1, source_target_pairs={{0,6},{1,7},{2,4},{3,5},{4,2},{5,3},{6,0},{7,1},{8,14},{9,15},{10,... | collective-permute-start | bytes 393224 | tf_op jit(solution)/shard_map/ppermute | solution.py:245
  116.5 2.3 %shard_map.75 = (f32[8,128]{1,0:T(8,128)S(1)}, f32[512,128]{1,0:T(8,128)S(1)}, f32[512,128]{1,0:T(8,128)S(1)}, f32[512,128]{1,0:T(8,128)S(1)}, f32[512,128]{1,0:T(8,128)S(1)}) custom-call(f32[8,128]{1,0:T(8,128)S(1)} %get-tuple-element.97.token_ref, bf16[2048,2048]{1,0:T(8,128)(2,1)S(1)} %copy-done.1, bf16[512,128]{1,0:T(8,128)(2,1)S(1)} %get-tuple-element.98.refs_0_, ...), custom_call_target="tpu_custom_call" | custom-call | tf_op jit(solution)/shard_map/pallas_call | solution.py:134
  118.9 1.6 %collective-permute-start.23 = (f16[512,256]{1,0:T(8,128)(2,1)S(1)}, f16[512,256]{1,0:T(8,128)(2,1)S(1)}, u32[]{:S(2)}, u32[]{:S(2)}) collective-permute-start(f16[512,256]{1,0:T(8,128)(2,1)S(1)} %fusion.2), channel_id=1, source_target_pairs={{0,8},{8,0},{16,24},{24,16},{1,9},{9,1},{17,25},{25,17},{2,10},{10... | collective-permute-start | bytes 786440 | tf_op jit(solution)/shard_map/ppermute | solution.py:245
  120.5 2.0 %collective-permute-done.36.refs_2_ = bf16[512,128]{1,0:T(8,128)(2,1)S(1)} collective-permute-done((bf16[512,128]{1,0:T(8,128)(2,1)S(1)}, bf16[512,128]{1,0:T(8,128)(2,1)S(1)}, u32[]{:S(2)}, u32[]{:S(2)}) %collective-permute-start.36) | collective-permute-done | bytes 131104 | tf_op jit(solution)/shard_map/ppermute | solution.py:245
  122.6 2.8 %shard_map.76 = (f32[8,128]{1,0:T(8,128)}, f32[512,128]{1,0:T(8,128)S(1)}, f32[512,128]{1,0:T(8,128)S(1)}, f32[512,128]{1,0:T(8,128)S(1)}, f32[512,128]{1,0:T(8,128)S(1)}) custom-call(f32[8,128]{1,0:T(8,128)S(1)} %get-tuple-element.103.token_ref, bf16[2048,2048]{1,0:T(8,128)(2,1)S(1)} %copy-done.1, bf16[512,128]{1,0:T(8,128)(2,1)S(1)} %get-tuple-element.104.refs_0_, ...), custom_call_target="tpu_custom_call" | custom-call | tf_op jit(solution)/shard_map/pallas_call | solution.py:134
  133.3 2.1 %collective-permute-done.39 = f16[512,128]{1,0:T(8,128)(2,1)S(1)} collective-permute-done((f16[512,128]{1,0:T(8,128)(2,1)S(1)}, f16[512,128]{1,0:T(8,128)(2,1)S(1)}, u32[]{:S(2)}, u32[]{:S(2)}) %collective-permute-start.39) | collective-permute-done | bytes 131104 | tf_op jit(solution)/shard_map/ppermute | solution.py:245
  136.0 1.7 %collective-permute-done.34 = f16[512,128]{1,0:T(8,128)(2,1)S(1)} collective-permute-done((f16[512,128]{1,0:T(8,128)(2,1)S(1)}, f16[512,128]{1,0:T(8,128)(2,1)S(1)}, u32[]{:S(2)}, u32[]{:S(2)}) %collective-permute-start.34) | collective-permute-done | bytes 131104 | tf_op jit(solution)/shard_map/ppermute | solution.py:245
  (150 shorter events, 40.6 us)
Async XLA Ops:
  0.0 11.6 %collective-permute-start.3 = (bf16[16,256,256]{2,1,0:T(8,128)(2,1)}, bf16[16,256,256]{2,1,0:T(8,128)(2,1)}, u32[]{:S(2)}, u32[]{:S(2)}) collective-permute-start(bf16[16,256,256]{2,1,0:T(8,128)(2,1)} %bitcast.39), channel_id=1, source_target_pairs={{0,1},{1,0},{2,3},{3,2},{4,5},{5,4},{6,7},{7,6},{8,9},{9,8},{10,11... | collective-permute-start | bytes 6291464 | tf_op jit(solution)/shard_map/ppermute | solution.py:245
  6.1 14.7 %collective-permute-start.4 = (bf16[512,256]{1,0:T(8,128)(2,1)S(1)}, bf16[512,256]{1,0:T(8,128)(2,1)S(1)}, u32[]{:S(2)}, u32[]{:S(2)}) collective-permute-start(bf16[512,256]{1,0:T(8,128)(2,1)S(1)} %get-tuple-element.60.refs_0_), channel_id=1, source_target_pairs={{0,2},{1,3},{2,0},{3,1},{4,6},{5,7},{6,4},{7,5},{8,10},{9,11},{10,... | collective-permute-start | bytes 786440 | tf_op jit(solution)/shard_map/ppermute | solution.py:245
  8.9 21.3 %collective-permute-start.5 = (bf16[512,256]{1,0:T(8,128)(2,1)S(1)}, bf16[512,256]{1,0:T(8,128)(2,1)S(1)}, u32[]{:S(2)}, u32[]{:S(2)}) collective-permute-start(bf16[512,256]{1,0:T(8,128)(2,1)S(1)} %get-tuple-element.60.refs_0_), channel_id=1, source_target_pairs={{0,4},{1,5},{2,6},{3,7},{4,0},{5,1},{6,2},{7,3},{8,12},{9,13},{10,... | collective-permute-start | bytes 786440 | tf_op jit(solution)/shard_map/ppermute | solution.py:245
  11.5 18.8 %collective-permute-start.6 = (bf16[512,256]{1,0:T(8,128)(2,1)S(1)}, bf16[512,256]{1,0:T(8,128)(2,1)S(1)}, u32[]{:S(2)}, u32[]{:S(2)}) collective-permute-start(bf16[512,256]{1,0:T(8,128)(2,1)S(1)} %get-tuple-element.60.refs_0_), channel_id=1, source_target_pairs={{0,6},{1,7},{2,4},{3,5},{4,2},{5,3},{6,0},{7,1},{8,14},{9,15},{10,... | collective-permute-start | bytes 786440 | tf_op jit(solution)/shard_map/ppermute | solution.py:245
  11.5 29.8 %collective-permute-start.7 = (f32[256,128]{1,0:T(8,128)S(1)}, f32[256,128]{1,0:T(8,128)S(1)}, u32[]{:S(2)}, u32[]{:S(2)}) collective-permute-start(f32[256,128]{1,0:T(8,128)S(1)} %get-tuple-element.116), channel_id=1, source_target_pairs={{0,1},{1,0},{2,3},{3,2},{4,5},{5,4},{6,7},{7,6},{8,9},{9,8},{10,11... | collective-permute-start | bytes 393224 | tf_op jit(solution)/shard_map/ppermute | solution.py:245
  32.5 25.7 %collective-permute-start.11 = (f32[520,256]{1,0:T(8,128)S(1)}, f32[520,256]{1,0:T(8,128)S(1)}, u32[]{:S(2)}, u32[]{:S(2)}) collective-permute-start(f32[520,256]{1,0:T(8,128)S(1)} %get-tuple-element.68), channel_id=1, source_target_pairs={{0,8},{8,0},{16,24},{24,16},{1,9},{9,1},{17,25},{25,17},{2,10},{10... | collective-permute-start | bytes 1597448 | tf_op jit(solution)/shard_map/ppermute | solution.py:245
  34.1 25.8 %collective-permute-start.12 = (f32[520,256]{1,0:T(8,128)S(1)}, f32[520,256]{1,0:T(8,128)S(1)}, u32[]{:S(2)}, u32[]{:S(2)}) collective-permute-start(f32[520,256]{1,0:T(8,128)S(1)} %get-tuple-element.69), channel_id=1, source_target_pairs={{0,16},{8,24},{16,0},{24,8},{1,17},{9,25},{17,1},{25,9},{2,18},{10... | collective-permute-start | bytes 1597448 | tf_op jit(solution)/shard_map/ppermute | solution.py:245
  35.6 25.8 %collective-permute-start.13 = (f32[520,256]{1,0:T(8,128)S(1)}, f32[520,256]{1,0:T(8,128)S(1)}, u32[]{:S(2)}, u32[]{:S(2)}) collective-permute-start(f32[520,256]{1,0:T(8,128)S(1)} %get-tuple-element.70), channel_id=1, source_target_pairs={{0,24},{8,16},{16,8},{24,0},{1,25},{9,17},{17,9},{25,1},{2,26},{10... | collective-permute-start | bytes 1597448 | tf_op jit(solution)/shard_map/ppermute | solution.py:245
  36.1 9.5 %collective-permute-start.8 = (bf16[512,128]{1,0:T(8,128)(2,1)S(1)}, bf16[512,128]{1,0:T(8,128)(2,1)S(1)}, u32[]{:S(2)}, u32[]{:S(2)}) collective-permute-start(bf16[512,128]{1,0:T(8,128)(2,1)S(1)} %get-tuple-element.64.refs_0_), channel_id=1, source_target_pairs={{0,2},{1,3},{2,0},{3,1},{4,6},{5,7},{6,4},{7,5},{8,10},{9,11},{10,... | collective-permute-start | bytes 393224 | tf_op jit(solution)/shard_map/ppermute | solution.py:245
  41.4 10.3 %collective-permute-start.9 = (bf16[512,128]{1,0:T(8,128)(2,1)S(1)}, bf16[512,128]{1,0:T(8,128)(2,1)S(1)}, u32[]{:S(2)}, u32[]{:S(2)}) collective-permute-start(bf16[512,128]{1,0:T(8,128)(2,1)S(1)} %get-tuple-element.64.refs_0_), channel_id=1, source_target_pairs={{0,4},{1,5},{2,6},{3,7},{4,0},{5,1},{6,2},{7,3},{8,12},{9,13},{10,... | collective-permute-start | bytes 393224 | tf_op jit(solution)/shard_map/ppermute | solution.py:245
  51.7 11.5 %collective-permute-start.14 = (bf16[512,128]{1,0:T(8,128)(2,1)S(1)}, bf16[512,128]{1,0:T(8,128)(2,1)S(1)}, u32[]{:S(2)}, u32[]{:S(2)}) collective-permute-start(bf16[512,128]{1,0:T(8,128)(2,1)S(1)} %get-tuple-element.74.refs_0_), channel_id=1, source_target_pairs={{0,2},{1,3},{2,0},{3,1},{4,6},{5,7},{6,4},{7,5},{8,10},{9,11},{10,... | collective-permute-start | bytes 393224 | tf_op jit(solution)/shard_map/ppermute | solution.py:245
  52.8 15.2 %collective-permute-start.15 = (bf16[512,128]{1,0:T(8,128)(2,1)S(1)}, bf16[512,128]{1,0:T(8,128)(2,1)S(1)}, u32[]{:S(2)}, u32[]{:S(2)}) collective-permute-start(bf16[512,128]{1,0:T(8,128)(2,1)S(1)} %get-tuple-element.74.refs_0_), channel_id=1, source_target_pairs={{0,4},{1,5},{2,6},{3,7},{4,0},{5,1},{6,2},{7,3},{8,12},{9,13},{10,... | collective-permute-start | bytes 393224 | tf_op jit(solution)/shard_map/ppermute | solution.py:245
  58.3 24.5 %collective-permute-start.17 = (f32[512,128]{1,0:T(8,128)S(1)}, f32[512,128]{1,0:T(8,128)S(1)}, u32[]{:S(2)}, u32[]{:S(2)}) collective-permute-start(f32[512,128]{1,0:T(8,128)S(1)} %get-tuple-element.78), channel_id=1, source_target_pairs={{0,8},{8,0},{16,24},{24,16},{1,9},{9,1},{17,25},{25,17},{2,10},{10... | collective-permute-start | bytes 786440 | tf_op jit(solution)/shard_map/ppermute | solution.py:245
  59.9 23.8 %collective-permute-start.18 = (f32[512,128]{1,0:T(8,128)S(1)}, f32[512,128]{1,0:T(8,128)S(1)}, u32[]{:S(2)}, u32[]{:S(2)}) collective-permute-start(f32[512,128]{1,0:T(8,128)S(1)} %get-tuple-element.79), channel_id=1, source_target_pairs={{0,16},{8,24},{16,0},{24,8},{1,17},{9,25},{17,1},{25,9},{2,18},{10... | collective-permute-start | bytes 786440 | tf_op jit(solution)/shard_map/ppermute | solution.py:245
  61.4 24.6 %collective-permute-start.19 = (f32[512,128]{1,0:T(8,128)S(1)}, f32[512,128]{1,0:T(8,128)S(1)}, u32[]{:S(2)}, u32[]{:S(2)}) collective-permute-start(f32[512,128]{1,0:T(8,128)S(1)} %get-tuple-element.80), channel_id=1, source_target_pairs={{0,24},{8,16},{16,8},{24,0},{1,25},{9,17},{17,9},{25,1},{2,26},{10... | collective-permute-start | bytes 786440 | tf_op jit(solution)/shard_map/ppermute | solution.py:245
  63.1 26.1 %collective-permute-start.20 = (bf16[512,256]{1,0:T(8,128)(2,1)}, bf16[512,256]{1,0:T(8,128)(2,1)S(1)}, u32[]{:S(2)}, u32[]{:S(2)}) collective-permute-start(bf16[512,256]{1,0:T(8,128)(2,1)} %get-tuple-element.82.refs_0_), channel_id=1, source_target_pairs={{0,2},{1,3},{2,0},{3,1},{4,6},{5,7},{6,4},{7,5},{8,10},{9,11},{10,... | collective-permute-start | bytes 786440 | tf_op jit(solution)/shard_map/ppermute | solution.py:245
  68.1 10.9 %collective-permute-start.16 = (bf16[512,128]{1,0:T(8,128)(2,1)S(1)}, bf16[512,128]{1,0:T(8,128)(2,1)S(1)}, u32[]{:S(2)}, u32[]{:S(2)}) collective-permute-start(bf16[512,128]{1,0:T(8,128)(2,1)S(1)} %get-tuple-element.74.refs_0_), channel_id=1, source_target_pairs={{0,6},{1,7},{2,4},{3,5},{4,2},{5,3},{6,0},{7,1},{8,14},{9,15},{10,... | collective-permute-start | bytes 393224 | tf_op jit(solution)/shard_map/ppermute | solution.py:245
  79.0 16.1 %collective-permute-start.21 = (bf16[512,256]{1,0:T(8,128)(2,1)}, bf16[512,256]{1,0:T(8,128)(2,1)}, u32[]{:S(2)}, u32[]{:S(2)}) collective-permute-start(bf16[512,256]{1,0:T(8,128)(2,1)} %get-tuple-element.82.refs_0_), channel_id=1, source_target_pairs={{0,4},{1,5},{2,6},{3,7},{4,0},{5,1},{6,2},{7,3},{8,12},{9,13},{10,... | collective-permute-start | bytes 786440 | tf_op jit(solution)/shard_map/ppermute | solution.py:245
  83.5 13.2 %collective-permute-start.22 = (bf16[512,256]{1,0:T(8,128)(2,1)}, bf16[512,256]{1,0:T(8,128)(2,1)}, u32[]{:S(2)}, u32[]{:S(2)}) collective-permute-start(bf16[512,256]{1,0:T(8,128)(2,1)} %get-tuple-element.82.refs_0_), channel_id=1, source_target_pairs={{0,6},{1,7},{2,4},{3,5},{4,2},{5,3},{6,0},{7,1},{8,14},{9,15},{10,... | collective-permute-start | bytes 786440 | tf_op jit(solution)/shard_map/ppermute | solution.py:245
  84.4 22.0 %collective-permute-start.26 = (f32[512,128]{1,0:T(8,128)}, f32[512,128]{1,0:T(8,128)}, u32[]{:S(2)}, u32[]{:S(2)}) collective-permute-start(f32[512,128]{1,0:T(8,128)} %get-tuple-element.94), channel_id=1, source_target_pairs={{0,8},{8,0},{16,24},{24,16},{1,9},{9,1},{17,25},{25,17},{2,10},{10... | collective-permute-start | bytes 786440 | tf_op jit(solution)/shard_map/ppermute | solution.py:245
  86.7 21.9 %collective-permute-start.27 = (f32[512,128]{1,0:T(8,128)}, f32[512,128]{1,0:T(8,128)}, u32[]{:S(2)}, u32[]{:S(2)}) collective-permute-start(f32[512,128]{1,0:T(8,128)} %get-tuple-element.95), channel_id=1, source_target_pairs={{0,16},{8,24},{16,0},{24,8},{1,17},{9,25},{17,1},{25,9},{2,18},{10... | collective-permute-start | bytes 786440 | tf_op jit(solution)/shard_map/ppermute | solution.py:245
  90.0 18.6 %collective-permute-start.28 = (f32[512,128]{1,0:T(8,128)}, f32[512,128]{1,0:T(8,128)}, u32[]{:S(2)}, u32[]{:S(2)}) collective-permute-start(f32[512,128]{1,0:T(8,128)} %get-tuple-element.96), channel_id=1, source_target_pairs={{0,24},{8,16},{16,8},{24,0},{1,25},{9,17},{17,9},{25,1},{2,26},{10... | collective-permute-start | bytes 786440 | tf_op jit(solution)/shard_map/ppermute | solution.py:245
  95.1 17.2 %collective-permute-start.29 = (bf16[512,128]{1,0:T(8,128)(2,1)S(1)}, bf16[512,128]{1,0:T(8,128)(2,1)S(1)}, u32[]{:S(2)}, u32[]{:S(2)}) collective-permute-start(bf16[512,128]{1,0:T(8,128)(2,1)S(1)} %get-tuple-element.98.refs_0_), channel_id=1, source_target_pairs={{0,2},{1,3},{2,0},{3,1},{4,6},{5,7},{6,4},{7,5},{8,10},{9,11},{10,... | collective-permute-start | bytes 393224 | tf_op jit(solution)/shard_map/ppermute | solution.py:245
  96.7 17.8 %collective-permute-start.30 = (bf16[512,128]{1,0:T(8,128)(2,1)S(1)}, bf16[512,128]{1,0:T(8,128)(2,1)S(1)}, u32[]{:S(2)}, u32[]{:S(2)}) collective-permute-start(bf16[512,128]{1,0:T(8,128)(2,1)S(1)} %get-tuple-element.98.refs_0_), channel_id=1, source_target_pairs={{0,4},{1,5},{2,6},{3,7},{4,0},{5,1},{6,2},{7,3},{8,12},{9,13},{10,... | collective-permute-start | bytes 393224 | tf_op jit(solution)/shard_map/ppermute | solution.py:245
  106.4 9.6 %collective-permute-start.31 = (bf16[512,128]{1,0:T(8,128)(2,1)S(1)}, bf16[512,128]{1,0:T(8,128)(2,1)S(1)}, u32[]{:S(2)}, u32[]{:S(2)}) collective-permute-start(bf16[512,128]{1,0:T(8,128)(2,1)S(1)} %get-tuple-element.98.refs_0_), channel_id=1, source_target_pairs={{0,6},{1,7},{2,4},{3,5},{4,2},{5,3},{6,0},{7,1},{8,14},{9,15},{10,... | collective-permute-start | bytes 393224 | tf_op jit(solution)/shard_map/ppermute | solution.py:245
  109.9 9.1 %collective-permute-start.35 = (bf16[512,128]{1,0:T(8,128)(2,1)S(1)}, bf16[512,128]{1,0:T(8,128)(2,1)S(1)}, u32[]{:S(2)}, u32[]{:S(2)}) collective-permute-start(bf16[512,128]{1,0:T(8,128)(2,1)S(1)} %get-tuple-element.104.refs_0_), channel_id=1, source_target_pairs={{0,2},{1,3},{2,0},{3,1},{4,6},{5,7},{6,4},{7,5},{8,10},{9,11},{10,... | collective-permute-start | bytes 393224 | tf_op jit(solution)/shard_map/ppermute | solution.py:245
  109.9 12.6 %collective-permute-start.36 = (bf16[512,128]{1,0:T(8,128)(2,1)S(1)}, bf16[512,128]{1,0:T(8,128)(2,1)S(1)}, u32[]{:S(2)}, u32[]{:S(2)}) collective-permute-start(bf16[512,128]{1,0:T(8,128)(2,1)S(1)} %get-tuple-element.104.refs_0_), channel_id=1, source_target_pairs={{0,4},{1,5},{2,6},{3,7},{4,0},{5,1},{6,2},{7,3},{8,12},{9,13},{10,... | collective-permute-start | bytes 393224 | tf_op jit(solution)/shard_map/ppermute | solution.py:245
  112.3 10.2 %collective-permute-start.37 = (bf16[512,128]{1,0:T(8,128)(2,1)S(1)}, bf16[512,128]{1,0:T(8,128)(2,1)S(1)}, u32[]{:S(2)}, u32[]{:S(2)}) collective-permute-start(bf16[512,128]{1,0:T(8,128)(2,1)S(1)} %get-tuple-element.104.refs_0_), channel_id=1, source_target_pairs={{0,6},{1,7},{2,4},{3,5},{4,2},{5,3},{6,0},{7,1},{8,14},{9,15},{10,... | collective-permute-start | bytes 393224 | tf_op jit(solution)/shard_map/ppermute | solution.py:245
  114.5 13.4 %collective-permute-start.25 = (f16[512,256]{1,0:T(8,128)(2,1)S(1)}, f16[512,256]{1,0:T(8,128)(2,1)S(1)}, u32[]{:S(2)}, u32[]{:S(2)}) collective-permute-start(f16[512,256]{1,0:T(8,128)(2,1)S(1)} %fusion.7), channel_id=1, source_target_pairs={{0,24},{8,16},{16,8},{24,0},{1,25},{9,17},{17,9},{25,1},{2,26},{10... | collective-permute-start | bytes 786440 | tf_op jit(solution)/shard_map/ppermute | solution.py:245
  116.1 13.3 %collective-permute-start.24 = (f16[512,256]{1,0:T(8,128)(2,1)S(1)}, f16[512,256]{1,0:T(8,128)(2,1)S(1)}, u32[]{:S(2)}, u32[]{:S(2)}) collective-permute-start(f16[512,256]{1,0:T(8,128)(2,1)S(1)} %fusion.6), channel_id=1, source_target_pairs={{0,16},{8,24},{16,0},{24,8},{1,17},{9,25},{17,1},{25,9},{2,18},{10... | collective-permute-start | bytes 786440 | tf_op jit(solution)/shard_map/ppermute | solution.py:245
  118.9 11.5 %collective-permute-start.23 = (f16[512,256]{1,0:T(8,128)(2,1)S(1)}, f16[512,256]{1,0:T(8,128)(2,1)S(1)}, u32[]{:S(2)}, u32[]{:S(2)}) collective-permute-start(f16[512,256]{1,0:T(8,128)(2,1)S(1)} %fusion.2), channel_id=1, source_target_pairs={{0,8},{8,0},{16,24},{24,16},{1,9},{9,1},{17,25},{25,17},{2,10},{10... | collective-permute-start | bytes 786440 | tf_op jit(solution)/shard_map/ppermute | solution.py:245
  126.5 8.9 %collective-permute-start.39 = (f16[512,128]{1,0:T(8,128)(2,1)S(1)}, f16[512,128]{1,0:T(8,128)(2,1)S(1)}, u32[]{:S(2)}, u32[]{:S(2)}) collective-permute-start(f16[512,128]{1,0:T(8,128)(2,1)S(1)} %get-tuple-element.131), channel_id=1, source_target_pairs={{0,16},{8,24},{16,0},{24,8},{1,17},{9,25},{17,1},{25,9},{2,18},{10... | collective-permute-start | bytes 393224 | tf_op jit(solution)/shard_map/ppermute | solution.py:245
  (30 other events, 170.8 us)

commit v2 on v1

v2 whole, which is shorter than its diff:
```python
import functools
import math

import jax
import jax.numpy as jnp
from jax import lax
from jax.experimental import pallas as pl
from jax.experimental.pallas import tpu as pltpu
from jax.sharding import PartitionSpec as P

SWEEPS = 2
PARTS = [1, 1]
FORWARD = 0
ORDER = ("A0", "A1", "G", "D0", "U0", "D1", "D2", "U1", "D3", "U2", "U3")
DENSE_LIMIT = 14
TERM_LIMIT = 14
UPDATE_LIMIT = 4
spread_weight = 0.8

COST = None
FREE = pl.CostEstimate(flops=0, bytes_accessed=0, transcendentals=0)
MIB = 1024 * 1024
LANES = 128
STEP = 235.0
SHIFT = 2.0**-62.5
PIN = 0
PIN_IN = 0


def dense_kernel(slot_ref, tiles_ref, near_tiles_ref, dense_ref, column_ref, *degree_refs):
    rows_n = slot_ref.shape[0]
    side = tiles_ref.shape[1]
    places = dense_ref.shape[1] // side
    ones = jnp.ones((8, dense_ref.shape[1]), dense_ref.dtype)
    ones_down = jnp.ones((dense_ref.shape[1], LANES), dense_ref.dtype)

    def line(i, _):
        for e, source in enumerate((tiles_ref, near_tiles_ref)):
            at = pl.ds(pl.multiple_of((e * rows_n + i) * side, side), side)
            for q in range(places):
                slot = slot_ref[i, e * places + q]
                tile = source[jnp.maximum(slot, 0)]
                dense_ref[at, q * side : (q + 1) * side] = jnp.where(slot >= 0, tile, jnp.zeros_like(tile))
            degree = lax.dot_general(
                ones, dense_ref[at], (((1,), (1,)), ((), ())), preferred_element_type=jnp.float32
            )
            for m, degree_ref in enumerate(degree_refs):

                @pl.when(i == m)
                def _():
                    for k in range(side // LANES):
                        to = e * (side // LANES) + k
                        degree_ref[to : to + 1] = degree[:1, k * LANES : (k + 1) * LANES]

            column_ref[at] = 1.0 / jnp.dot(dense_ref[at], ones_down, preferred_element_type=jnp.float32)
        return 0

    lax.fori_loop(0, rows_n, line, 0)


def dense_tiles(table, tiles, near_tiles):
    rows_n, places = table.shape
    side = tiles.shape[1]
    dense = jax.ShapeDtypeStruct((2 * rows_n * side, places // 2 * side), tiles.dtype)
    if PIN and dense.size * 2 <= 8 * MIB:
        dense = pltpu.VMEM(dense.shape, dense.dtype)
    return pl.pallas_call(
        dense_kernel,
        out_shape=[
            dense,
            jax.ShapeDtypeStruct((2 * rows_n * side, LANES), jnp.float32),
        ]
        + [jax.ShapeDtypeStruct((-(-2 * side // LANES // 8) * 8, LANES), jnp.float32)] * rows_n,
        in_specs=[pl.BlockSpec(memory_space=pltpu.SMEM)] + [pl.BlockSpec(memory_space=pltpu.VMEM)] * 2,
        out_specs=[pl.BlockSpec(memory_space=pltpu.VMEM)] * (2 + rows_n),
        compiler_params=pltpu.CompilerParams(vmem_limit_bytes=(DENSE_LIMIT if dense.shape[0] * dense.shape[1] <= 4 * MIB else 56) * MIB),
        cost_estimate=FREE,
    )(table, tiles, near_tiles)


def encode(value, inverse, code_ref, rows, scale_rows):
    lanes = [slice(at, at + LANES) for at in range(0, value.shape[1], LANES)]
    parts = [value[:, at] * inverse for at in lanes]
    top = jnp.max(functools.reduce(jnp.maximum, parts), axis=(0, 1), keepdims=True)
    top = jnp.broadcast_to(jnp.maximum(top, 1e-30), (16, LANES)).astype(jnp.bfloat16)
    factor = STEP / top.astype(jnp.float32)[:1]
    for at, part in zip(lanes, parts):
        power = 1.0 + part * factor
        for _ in range(4):
            power = power * power
        power = power * SHIFT
        code_ref[rows, at] = (power * power).astype(jnp.bfloat16)
        code_ref[scale_rows, at] = top


def decode(code_ref, rows, scale_row, at):
    top = code_ref[scale_row : scale_row + 16, at].astype(jnp.float32)[:1]
    power = jnp.log(code_ref[rows, at].astype(jnp.float32)) - 2.0 * math.log(SHIFT)
    return (jnp.exp(power * (1.0 / 32.0)) - 1.0) * (top * (1.0 / STEP))


def term_kernel(count, rows_n, token_ref, dense_ref, inverse_ref, *refs):
    block_refs, (next_ref, own_ref, *code_refs) = refs[:count], refs[count:]
    next_ref[...] = token_ref[...]
    blocks = [r[...] for r in block_refs]
    if count == 5:
        blocks = blocks[:3] + [blocks[3] + blocks[4]]
    depth = blocks[0].shape[0]
    side = depth // 2
    for e in range(2):
        lines = slice(e * rows_n * side, (e + 1) * rows_n * side)
        total = None
        for k, block in enumerate(blocks):
            product = jnp.dot(
                dense_ref[lines, k * depth : (k + 1) * depth], block, preferred_element_type=jnp.float32
            )
            total = product if total is None else total + product
        rows = slice(e * side, (e + 1) * side)
        own_ref[rows] = total[:side]
        for m, code_ref in enumerate(code_refs, 1):
            line = slice((e * rows_n + m) * side, (e * rows_n + m + 1) * side)
            scale_rows = slice(depth + 16 * e, depth + 16 * (e + 1))
            encode(total[m * side : (m + 1) * side], inverse_ref[line], code_ref, rows, scale_rows)


def term_step_kernel(count, rows_n, token_ref, dense_ref, inverse_ref, *refs):
    block_refs, (next_ref, own_ref, *code_refs) = refs[:count], refs[count:]
    next_ref[...] = token_ref[...]
    depth = block_refs[0].shape[0]
    side = depth // 2
    e, line = pl.program_id(0), pl.program_id(1)
    total = None
    for k, block_ref in enumerate(block_refs):
        product = jnp.dot(
            dense_ref[:, k * depth : (k + 1) * depth], block_ref[...], preferred_element_type=jnp.float32
        )
        total = product if total is None else total + product
    rows = pl.ds(pl.multiple_of(e * side, side), side)
    scale_rows = pl.ds(pl.multiple_of(depth + 16 * e, 16), 16)

    @pl.when(line == 0)
    def _():
        own_ref[rows] = total

    for m, code_ref in enumerate(code_refs, 1):

        @pl.when(line == m)
        def _():
            encode(total, inverse_ref[...], code_ref, rows, scale_rows)


def terms(token, dense, inverse, blocks, rows_n):
    side = dense.shape[0] // (2 * rows_n)
    width = blocks[0].shape[1]
    whole = dense.size * 2 <= 8 * MIB
    vmem = pl.BlockSpec(memory_space=pltpu.VMEM)
    own = jax.ShapeDtypeStruct((2 * side, width), jnp.float32)
    code = jax.ShapeDtypeStruct((2 * side + 32, width), jnp.bfloat16)
    if whole and PIN_IN:
        dense = pltpu.with_memory_space_constraint(dense, pltpu.VMEM)
    if whole:
        split = dict(in_specs=[vmem] * (3 + len(blocks)), out_specs=[vmem] * (1 + rows_n))
    else:
        at_start = lambda x: pl.BlockSpec(x.shape, lambda e, m: (0, 0))
        split = dict(
            grid=(2, rows_n),
            in_specs=[
                at_start(token),
                pl.BlockSpec((side, dense.shape[1]), lambda e, m: (e * rows_n + m, 0)),
                pl.BlockSpec((side, LANES), lambda e, m: (e * rows_n + m, 0)),
            ]
            + [at_start(x) for x in blocks],
            out_specs=[at_start(token), at_start(own)] + [at_start(code)] * (rows_n - 1),
        )
    token, *out = pl.pallas_call(
        functools.partial(term_kernel if whole else term_step_kernel, len(blocks), rows_n),
        out_shape=[jax.ShapeDtypeStruct(token.shape, token.dtype), own] + [code] * (rows_n - 1),
        compiler_params=pltpu.CompilerParams(vmem_limit_bytes=(TERM_LIMIT if whole else 48) * MIB),
        cost_estimate=FREE,
        **split,
    )(token, dense, inverse, *blocks)
    return token, out


def after(token, waited):
    anywhere = pl.BlockSpec(memory_space=pl.ANY)
    vmem = pl.BlockSpec(memory_space=pltpu.VMEM)

    def kernel(token_ref, waited_ref, next_ref):
        next_ref[...] = token_ref[...]

    return pl.pallas_call(
        kernel,
        out_shape=jax.ShapeDtypeStruct(token.shape, token.dtype),
        in_specs=[vmem, anywhere],
        out_specs=vmem,
        compiler_params=pltpu.CompilerParams(vmem_limit_bytes=MIB),
        cost_estimate=FREE,
    )(token, waited)


def begin_kernel(token_ref, kept_ref, got_ref, next_ref, prior_ref, coarse_ref):
    side = kept_ref.shape[0]
    next_ref[...] = token_ref[...]
    for k, ref in enumerate((kept_ref, got_ref)):
        prior_ref[k * side : (k + 1) * side] = ref[...]
        coarse_ref[k * side : (k + 1) * side] = ref[...].astype(jnp.bfloat16)


def begin(token, kept, got):
    rows, width = 2 * kept.shape[0], kept.shape[1]
    vmem = pl.BlockSpec(memory_space=pltpu.VMEM)
    return pl.pallas_call(
        begin_kernel,
        out_shape=[
            jax.ShapeDtypeStruct(token.shape, token.dtype),
            jax.ShapeDtypeStruct((rows, width), jnp.float32),
            jax.ShapeDtypeStruct((rows, width), jnp.bfloat16),
        ],
        in_specs=[vmem] * 3,
        out_specs=[vmem] * 3,
        compiler_params=pltpu.CompilerParams(vmem_limit_bytes=UPDATE_LIMIT * MIB),
        cost_estimate=FREE,
    )(token, kept, got)


def update_kernel(count, token_ref, keep_ref, scale_ref, prior_ref, own_ref, *refs):
    code_refs, degree_refs, (next_ref, out_ref) = refs[:count], refs[count : 2 * count], refs[2 * count :]
    next_ref[...] = token_ref[...]
    depth, width = out_ref.shape
    side = depth // 2
    for e in range(2):
        rows = slice(e * side, (e + 1) * side)
        for at in range(0, width, LANES):
            lanes = slice(at, at + LANES)
            summed = own_ref[rows, lanes]
            for code_ref, degree_ref in zip(code_refs, degree_refs):
                summed += decode(code_ref, rows, depth + 16 * e, lanes) * degree_ref[rows]
            prior = prior_ref[rows, lanes]
            value = scale_ref[rows] * summed + (1.0 - spread_weight) * prior
            out_ref[rows, lanes] = jnp.where(keep_ref[rows] > 0, prior, value).astype(out_ref.dtype)


def update(token, keep, scale, prior, own, codes, degrees, dtype):
    vmem = pl.BlockSpec(memory_space=pltpu.VMEM)
    return pl.pallas_call(
        functools.partial(update_kernel, len(codes)),
        out_shape=[
            jax.ShapeDtypeStruct(token.shape, token.dtype),
            jax.ShapeDtypeStruct(prior.shape, dtype),
        ],
        in_specs=[vmem] * (5 + 2 * len(codes)),
        out_specs=[vmem] * 2,
        compiler_params=pltpu.CompilerParams(vmem_limit_bytes=2 * UPDATE_LIMIT * MIB),
        cost_estimate=FREE,
    )(token, keep, scale, prior, own, *codes, *degrees)


def columns_kernel(token_ref, labelled_ref, *refs):
    row_refs, (next_ref, keep_ref, scale_ref, *column_refs) = refs[: len(refs) // 2 - 1], refs[len(refs) // 2 - 1 :]
    next_ref[...] = token_ref[...]

    def turn(ref, out_ref):
        for k in range(out_ref.shape[0] // LANES):
            flat = jnp.broadcast_to(ref[k : k + 1], (LANES, LANES))
            out_ref[k * LANES : (k + 1) * LANES] = flat.T

    turn(labelled_ref, keep_ref)
    turn(row_refs[0], scale_ref)
    total = scale_ref[...]
    for row_ref, column_ref in zip(row_refs[1:], column_refs):
        turn(row_ref, column_ref)
        total += column_ref[...]
    scale_ref[...] = spread_weight / total


def columns(token, labelled, rows, depth):
    vmem = pl.BlockSpec(memory_space=pltpu.VMEM)
    return pl.pallas_call(
        columns_kernel,
        out_shape=[jax.ShapeDtypeStruct(token.shape, token.dtype)]
        + [jax.ShapeDtypeStruct((depth, LANES), jnp.float32)] * (1 + len(rows)),
        in_specs=[vmem] * (2 + len(rows)),
        out_specs=[vmem] * (2 + len(rows)),
        compiler_params=pltpu.CompilerParams(vmem_limit_bytes=UPDATE_LIMIT * MIB),
        cost_estimate=FREE,
    )(token, labelled, *rows)


def swap(x, axis, mask):
    size = lax.axis_size(axis)
    return lax.ppermute(x, axis, [(i, i ^ mask) for i in range(size)])


def on_device(affinity, block_rows, block_cols, block_count, labels, labelled):
    tiles = affinity[0, 0]
    rows_n = lax.axis_size("row")
    cols_n = lax.axis_size("col")
    slots, side, _ = tiles.shape
    half = labels.shape[1] // 2
    row, col = lax.axis_index("row"), lax.axis_index("col")
    core = col & 1

    count = len(PARTS)
    widths = [half * p // sum(PARTS) for p in PARTS]
    starts = [sum(widths[:i]) for i in range(count)]
    halves = []
    for s, w in zip(starts, widths):
        kept = lax.dynamic_slice_in_dim(labels, core * half + s, w, 1)
        given = lax.dynamic_slice_in_dim(labels, (1 - core) * half + s, w, 1)
        halves.append((kept, swap(given, "col", 1)))

    live = jnp.arange(slots) < block_count[0, 0]
    hit = (
        ((block_rows[0, 0] ^ row)[None, None, :] == jnp.arange(rows_n)[:, None, None])
        & ((block_cols[0, 0] ^ col)[None, None, :] == jnp.arange(cols_n)[None, :, None])
        & live[None, None, :]
    )
    table = jnp.max(jnp.where(hit, jnp.arange(slots), -1), axis=2).astype(jnp.int32)
    near_tiles = swap(tiles, "col", 1)
    numbers = jnp.concatenate([table.reshape(-1), labelled])
    near_numbers = swap(numbers, "col", 1)
    near_table = near_numbers[: rows_n * cols_n].reshape(rows_n, cols_n // 2, 2)
    near_table = near_table[:, :, ::-1].reshape(rows_n, cols_n)
    table = jnp.concatenate([table, near_table], axis=1)
    both = jnp.concatenate([labelled, near_numbers[rows_n * cols_n :]])
    both = jnp.pad((both == 1).astype(jnp.float32).reshape(-1, LANES), ((0, -(2 * side // LANES) % 8), (0, 0)))
    inner = [i for i in range(cols_n) if (i >> 1) & 3 in (1, 2)]

    dense, inverse, *part = dense_tiles(table, tiles, near_tiles)
    part = [part[0]] + [swap(part[m], "row", m) for m in range(1, rows_n)]
    token = start = jnp.zeros((8, 128), jnp.float32)
    priors, held, sums, final = {}, {}, {}, {}

    def spread_out(x):
        if FORWARD:
            far = swap(x, "col", 4)
            blocks = [
                x,
                swap(x, "col", 2),
                far,
                lax.ppermute(x, "col", [(i, i ^ 6) for i in inner]),
                lax.ppermute(far, "col", [(i, i ^ 2) for i in inner]),
            ]
            if cols_n > 8:
                blocks = blocks[:3] + [blocks[3] + blocks[4]]
        else:
            blocks = [x] + [swap(x, "col", 2 * k) for k in range(1, min(4, cols_n // 2))]
        while 4 <= len(blocks) < cols_n // 2:
            blocks = blocks + [swap(b, "col", 2 * len(blocks)) for b in blocks]
        return blocks

    for name in ORDER:
        if name == "G":
            token, keep, scale, *degrees = columns(token, both, part, 2 * side)
            continue
        kind, n = name[0], int(name[1:].split(".")[0])
        c, last = n % count, n >= count * (SWEEPS - 1)
        free, token = token, (start if kind.islower() else token)
        kind = kind.upper()
        if kind == "W":
            token = after(token, held[n][int(name.split(".")[1])])
        elif kind == "A":
            token, priors[c], coarse = begin(token, *halves[c])
            held[n] = spread_out(coarse)
        elif kind == "D":
            token, (own, *codes) = terms(token, dense, inverse, held.pop(n), rows_n)
            sums[n] = own, [swap(x, "row", m) for m, x in enumerate(codes, 1)]
        else:
            dtype = jnp.float32 if last else jnp.bfloat16
            token, out = update(token, keep, scale, priors[c], *sums.pop(n), degrees, dtype)
            if last:
                final[c] = out[:side], swap(out[side:], "col", 1)
            else:
                held[n + count] = spread_out(out)
        if name[0].islower():
            token = free
    final = [final[c] for c in range(count)]
    mine, other = (jnp.concatenate([f[k] for f in final], axis=1) for k in (0, 1))
    low, high = jnp.where(core == 0, mine, other), jnp.where(core == 0, other, mine)
    return jnp.concatenate([low, high], axis=1)


def solution(mesh):
    placed = (
        P("row", "col", None, None, None),
        P("row", "col", None),
        P("row", "col", None),
        P("row", "col"),
        P(("row", "col"), None),
        P(("row", "col")),
    )
    return jax.shard_map(
        on_device, mesh=mesh, in_specs=placed, out_specs=P(("row", "col"), None), check_vma=False
    )
```

time: 143 us -> 127 us (0.89)
  starting transfers between devices: 58.8 us -> 45.3 us
  local copies, waits for them, and re-layouts: 15.3 us -> 2.69 us
  waiting for transfers between devices: 38.4 us -> 49.3 us
    ppermute x44 -> x33, starting transfers between devices: 58.8 us -> 45.3 us  [swap(): return lax.ppermute(x, axis, [(i, i ^ mask) for i in range(size)])]
    unnamed x39 -> x9, local copies, waits for them, and re-layouts: 12.4 us -> 0.04 us
    ppermute x44 -> x33, waiting for transfers between devices: 38.4 us -> 49.3 us  [swap(): return lax.ppermute(x, axis, [(i, i ^ mask) for i in range(size)])]
    pallas_call x1, Pallas kernels: 6.65 us -> 11.7 us  [dense_tiles(): pl.pallas_call(dense_kernel, out_shape=[dense, jax.ShapeDtypeStruct((2 *...]
    pallas_call x6 -> x4, Pallas kernels: 16.3 us -> 11.7 us  [terms(): pl.pallas_call(functools.partial(term_kernel if whole else term_step_kern...]
    pallas_call x3 -> x5, Pallas kernels: 2.63 us -> 3.26 us  [the longest x4 2.85 us: update(): pl.pallas_call(functools.partial(update_kernel, len(codes)), out_shape=[j...]
  transfers between devices with their start and end apart: 44 -> 33, of which waited for: 17 -> 15; matrix products, arithmetic and copies ran while one was open for 3% -> 2% of each run, Pallas kernels for 18% -> 18%
where the time goes in v2:
time: 127 us
  waiting for transfers between devices  49.3 us (39%)
  starting transfers between devices  45.3 us (36%)
  Pallas kernels  26.8 us (21%)
  local copies, waits for them, and re-layouts  2.69 us (2%)
  other arithmetic  1.54 us (1%)
    ppermute x33, waiting for transfers between devices, swap(): return lax.ppermute(x, axis, [(i, i ^ mask) for i in range(size)])  49.3 us
    ppermute x33, starting transfers between devices, swap(): return lax.ppermute(x, axis, [(i, i ^ mask) for i in range(size)])  45.3 us
    pallas_call x4, Pallas kernels, terms(): pl.pallas_call(functools.partial(term_kernel if whole else term_step_kern...  11.7 us
    pallas_call x1, Pallas kernels, dense_tiles(): pl.pallas_call(dense_kernel, out_shape=[dense, jax.ShapeDtypeStruct((2 *...  11.7 us
    pallas_call x4, Pallas kernels, update(): pl.pallas_call(functools.partial(update_kernel, len(codes)), out_shape=[j...  2.85 us
  transfers between devices with their start and end apart: 33, of which 15 were waited for; matrix products, arithmetic and copies ran while one was open for 2% of the time, Pallas kernels for 18%

profile of v2, /device:TPU:0, one launch (start us, length us, event | category | flops | bytes accessed | tf_op | source)
XLA Modules:
  0.0 126.6 jit_solution(18039745637219655658)
XLA Ops:
  0.5 2.0 %constant_dynamic-slice_fusion = (f32[256,256]{1,0:T(8,128)S(1)}, f32[256,256]{1,0:T(8,128)}, f32[256,256]{1,0:T(8,128)S(1)}, f32[256,256]{1,0:T(8,128)S(1)}) fusion(f32[256,1024]{1,0:T(8,128)} %param.10, s32[]{:T(128)S(6)} %select_n.32, s32[]{:T(128)S(6)} %select_n.30, s32[]{:T(128)S(6)} %select_n.29, s32[]{:T(128)S(6)} %select_n.31), kind=kLoop, calls=%fused_computation.14 | loop fusion | bytes 2097168 | tf_op jit(solution)/shard_map/dynamic_slice | solution.py:310
  5.5 5.0 %collective-permute-start.9 = (bf16[512,256]{1,0:T(8,128)(2,1)S(1)}, bf16[512,256]{1,0:T(8,128)(2,1)S(1)}, u32[]{:S(2)}, u32[]{:S(2)}) collective-permute-start(bf16[512,256]{1,0:T(8,128)(2,1)S(1)} %get-tuple-element.59.refs_0_), channel_id=1, source_target_pairs={{0,6},{1,7},{2,4},{3,5},{4,2},{5,3},{6,0},{7,1},{8,14},{9,15},{10,... | collective-permute-start | bytes 786440 | tf_op jit(solution)/shard_map/ppermute | solution.py:292
  11.2 11.7 %shard_map.66 = (bf16[2048,2048]{1,0:T(8,128)(2,1)S(1)}, f32[2048,128]{1,0:T(8,128)S(1)}, f32[8,128]{1,0:T(8,128)S(1)}, f32[8,128]{1,0:T(8,128)S(1)}, f32[8,128]{1,0:T(8,128)S(1)}, /*index=5*/f32[8,128]{1,0:T(8,128)S(1)}) custom-call(s32[4,16]{1,0:T(4,128)S(1)} %pad_add_fusion.1.slot_ref, bf16[16,256,256]{2,1,0:T(8,128)(2,1)S(1)} %bitcast.12, ...), custom_call_target="tpu_custom_call" | custom-call | tf_op jit(solution)/shard_map/pallas_call | solution.py:67
  22.9 1.7 %collective-permute-start.4 = (f32[8,128]{1,0:T(8,128)S(1)}, f32[8,128]{1,0:T(8,128)S(1)}, u32[]{:S(2)}, u32[]{:S(2)}) collective-permute-start(f32[8,128]{1,0:T(8,128)S(1)} %get-tuple-element.53), channel_id=1, source_target_pairs={{0,8},{8,0},{16,24},{24,16},{1,9},{9,1},{17,25},{25,17},{2,10},{10... | collective-permute-start | bytes 12296 | tf_op jit(solution)/shard_map/ppermute | solution.py:292
  24.6 1.6 %collective-permute-start.5 = (f32[8,128]{1,0:T(8,128)S(1)}, f32[8,128]{1,0:T(8,128)S(1)}, u32[]{:S(2)}, u32[]{:S(2)}) collective-permute-start(f32[8,128]{1,0:T(8,128)S(1)} %get-tuple-element.54), channel_id=1, source_target_pairs={{0,16},{8,24},{16,0},{24,8},{1,17},{9,25},{17,1},{25,9},{2,18},{10... | collective-permute-start | bytes 12296 | tf_op jit(solution)/shard_map/ppermute | solution.py:292
  26.6 2.6 %collective-permute-start.6 = (f32[8,128]{1,0:T(8,128)S(1)}, f32[8,128]{1,0:T(8,128)S(1)}, u32[]{:S(2)}, u32[]{:S(2)}) collective-permute-start(f32[8,128]{1,0:T(8,128)S(1)} %get-tuple-element.55), channel_id=1, source_target_pairs={{0,24},{8,16},{16,8},{24,0},{1,25},{9,17},{17,9},{25,1},{2,26},{10... | collective-permute-start | bytes 12296 | tf_op jit(solution)/shard_map/ppermute | solution.py:292
  29.2 1.8 %collective-permute-done.6.refs_3_ = f32[8,128]{1,0:T(8,128)S(1)} collective-permute-done((f32[8,128]{1,0:T(8,128)S(1)}, f32[8,128]{1,0:T(8,128)S(1)}, u32[]{:S(2)}, u32[]{:S(2)}) %collective-permute-start.6) | collective-permute-done | bytes 4128 | tf_op jit(solution)/shard_map/ppermute | solution.py:292
  31.5 1.6 %collective-permute-done.8.refs_2_ = bf16[512,256]{1,0:T(8,128)(2,1)S(1)} collective-permute-done((bf16[512,256]{1,0:T(8,128)(2,1)S(1)}, bf16[512,256]{1,0:T(8,128)(2,1)S(1)}, u32[]{:S(2)}, u32[]{:S(2)}) %collective-permute-start.8) | collective-permute-done | bytes 262176 | tf_op jit(solution)/shard_map/ppermute | solution.py:292
  33.1 2.9 %shard_map.68 = (f32[8,128]{1,0:T(8,128)S(1)}, f32[512,256]{1,0:T(8,128)S(1)}, bf16[544,256]{1,0:T(8,128)(2,1)S(1)}, bf16[544,256]{1,0:T(8,128)(2,1)S(1)}, bf16[544,256]{1,0:T(8,128)(2,1)S(1)}) custom-call(f32[8,128]{1,0:T(8,128)S(1)} %get-tuple-element.56.token_ref, bf16[2048,2048]{1,0:T(8,128)(2,1)S(1)} %get-tuple-element.57.dense_ref, ...), custom_call_target="tpu_custom_call" | custom-call | tf_op jit(solution)/shard_map/pallas_call | solution.py:175
  36.1 1.6 %collective-permute-start.10 = (bf16[544,256]{1,0:T(8,128)(2,1)S(1)}, bf16[544,256]{1,0:T(8,128)(2,1)S(1)}, u32[]{:S(2)}, u32[]{:S(2)}) collective-permute-start(bf16[544,256]{1,0:T(8,128)(2,1)S(1)} %get-tuple-element.65), channel_id=1, source_target_pairs={{0,8},{8,0},{16,24},{24,16},{1,9},{9,1},{17,25},{25,17},{2,10},{10... | collective-permute-start | bytes 835592 | tf_op jit(solution)/shard_map/ppermute | solution.py:292
  37.6 1.5 %collective-permute-start.11 = (bf16[544,256]{1,0:T(8,128)(2,1)S(1)}, bf16[544,256]{1,0:T(8,128)(2,1)S(1)}, u32[]{:S(2)}, u32[]{:S(2)}) collective-permute-start(bf16[544,256]{1,0:T(8,128)(2,1)S(1)} %get-tuple-element.66), channel_id=1, source_target_pairs={{0,16},{8,24},{16,0},{24,8},{1,17},{9,25},{17,1},{25,9},{2,18},{10... | collective-permute-start | bytes 835592 | tf_op jit(solution)/shard_map/ppermute | solution.py:292
  39.6 2.5 %collective-permute-start.15 = (bf16[512,256]{1,0:T(8,128)(2,1)S(1)}, bf16[512,256]{1,0:T(8,128)(2,1)S(1)}, u32[]{:S(2)}, u32[]{:S(2)}) collective-permute-start(bf16[512,256]{1,0:T(8,128)(2,1)S(1)} %get-tuple-element.72.refs_0_), channel_id=1, source_target_pairs={{0,6},{1,7},{2,4},{3,5},{4,2},{5,3},{6,0},{7,1},{8,14},{9,15},{10,... | collective-permute-start | bytes 786440 | tf_op jit(solution)/shard_map/ppermute | solution.py:292
  42.1 3.6 %collective-permute-done.10.refs_0_ = bf16[544,256]{1,0:T(8,128)(2,1)S(1)} collective-permute-done((bf16[544,256]{1,0:T(8,128)(2,1)S(1)}, bf16[544,256]{1,0:T(8,128)(2,1)S(1)}, u32[]{:S(2)}, u32[]{:S(2)}) %collective-permute-start.10) | collective-permute-done | bytes 278560 | tf_op jit(solution)/shard_map/ppermute | solution.py:292
  45.7 5.5 %collective-permute-done.11.refs_1_ = bf16[544,256]{1,0:T(8,128)(2,1)S(1)} collective-permute-done((bf16[544,256]{1,0:T(8,128)(2,1)S(1)}, bf16[544,256]{1,0:T(8,128)(2,1)S(1)}, u32[]{:S(2)}, u32[]{:S(2)}) %collective-permute-start.11) | collective-permute-done | bytes 278560 | tf_op jit(solution)/shard_map/ppermute | solution.py:292
  51.9 2.5 %collective-permute-start.18 = (bf16[512,256]{1,0:T(8,128)(2,1)S(1)}, bf16[512,256]{1,0:T(8,128)(2,1)S(1)}, u32[]{:S(2)}, u32[]{:S(2)}) collective-permute-start(bf16[512,256]{1,0:T(8,128)(2,1)S(1)} %get-tuple-element.74.refs_0_), channel_id=1, source_target_pairs={{0,6},{1,7},{2,4},{3,5},{4,2},{5,3},{6,0},{7,1},{8,14},{9,15},{10,... | collective-permute-start | bytes 786440 | tf_op jit(solution)/shard_map/ppermute | solution.py:292
  54.5 16.1 %collective-permute-done.14.refs_2_ = bf16[512,256]{1,0:T(8,128)(2,1)S(1)} collective-permute-done((bf16[512,256]{1,0:T(8,128)(2,1)S(1)}, bf16[512,256]{1,0:T(8,128)(2,1)S(1)}, u32[]{:S(2)}, u32[]{:S(2)}) %collective-permute-start.14) | collective-permute-done | bytes 262176 | tf_op jit(solution)/shard_map/ppermute | solution.py:292
  70.6 2.9 %shard_map.70 = (f32[8,128]{1,0:T(8,128)S(1)}, f32[512,256]{1,0:T(8,128)S(1)}, bf16[544,256]{1,0:T(8,128)(2,1)S(1)}, bf16[544,256]{1,0:T(8,128)(2,1)S(1)}, bf16[544,256]{1,0:T(8,128)(2,1)S(1)}) custom-call(f32[8,128]{1,0:T(8,128)S(1)} %get-tuple-element.71.token_ref, bf16[2048,2048]{1,0:T(8,128)(2,1)S(1)} %get-tuple-element.57.dense_ref, ...), custom_call_target="tpu_custom_call" | custom-call | tf_op jit(solution)/shard_map/pallas_call | solution.py:175
  73.5 1.6 %collective-permute-start.19 = (bf16[544,256]{1,0:T(8,128)(2,1)S(1)}, bf16[544,256]{1,0:T(8,128)(2,1)S(1)}, u32[]{:S(2)}, u32[]{:S(2)}) collective-permute-start(bf16[544,256]{1,0:T(8,128)(2,1)S(1)} %get-tuple-element.78), channel_id=1, source_target_pairs={{0,8},{8,0},{16,24},{24,16},{1,9},{9,1},{17,25},{25,17},{2,10},{10... | collective-permute-start | bytes 835592 | tf_op jit(solution)/shard_map/ppermute | solution.py:292
  75.1 1.5 %collective-permute-start.20 = (bf16[544,256]{1,0:T(8,128)(2,1)S(1)}, bf16[544,256]{1,0:T(8,128)(2,1)S(1)}, u32[]{:S(2)}, u32[]{:S(2)}) collective-permute-start(bf16[544,256]{1,0:T(8,128)(2,1)S(1)} %get-tuple-element.79), channel_id=1, source_target_pairs={{0,16},{8,24},{16,0},{24,8},{1,17},{9,25},{17,1},{25,9},{2,18},{10... | collective-permute-start | bytes 835592 | tf_op jit(solution)/shard_map/ppermute | solution.py:292
  77.1 2.5 %collective-permute-start.16 = (bf16[512,256]{1,0:T(8,128)(2,1)S(1)}, bf16[512,256]{1,0:T(8,128)(2,1)S(1)}, u32[]{:S(2)}, u32[]{:S(2)}) collective-permute-start(bf16[512,256]{1,0:T(8,128)(2,1)S(1)} %get-tuple-element.74.refs_0_), channel_id=1, source_target_pairs={{0,2},{1,3},{2,0},{3,1},{4,6},{5,7},{6,4},{7,5},{8,10},{9,11},{10,... | collective-permute-start | bytes 786440 | tf_op jit(solution)/shard_map/ppermute | solution.py:292
  79.6 7.4 %collective-permute-done.17.refs_2_ = bf16[512,256]{1,0:T(8,128)(2,1)S(1)} collective-permute-done((bf16[512,256]{1,0:T(8,128)(2,1)S(1)}, bf16[512,256]{1,0:T(8,128)(2,1)S(1)}, u32[]{:S(2)}, u32[]{:S(2)}) %collective-permute-start.17) | collective-permute-done | bytes 262176 | tf_op jit(solution)/shard_map/ppermute | solution.py:292
  87.0 2.9 %shard_map.71 = (f32[8,128]{1,0:T(8,128)S(1)}, f32[512,256]{1,0:T(8,128)S(1)}, bf16[544,256]{1,0:T(8,128)(2,1)S(1)}, bf16[544,256]{1,0:T(8,128)(2,1)S(1)}, bf16[544,256]{1,0:T(8,128)(2,1)S(1)}) custom-call(f32[8,128]{1,0:T(8,128)S(1)} %get-tuple-element.73.token_ref, bf16[2048,2048]{1,0:T(8,128)(2,1)S(1)} %get-tuple-element.57.dense_ref, ...), custom_call_target="tpu_custom_call" | custom-call | tf_op jit(solution)/shard_map/pallas_call | solution.py:175
  90.7 8.2 %collective-permute-start.24 = (bf16[512,256]{1,0:T(8,128)(2,1)S(1)}, bf16[512,256]{1,0:T(8,128)(2,1)S(1)}, u32[]{:S(2)}, u32[]{:S(2)}) collective-permute-start(bf16[512,256]{1,0:T(8,128)(2,1)S(1)} %get-tuple-element.82.refs_0_), channel_id=1, source_target_pairs={{0,6},{1,7},{2,4},{3,5},{4,2},{5,3},{6,0},{7,1},{8,14},{9,15},{10,... | collective-permute-start | bytes 786440 | tf_op jit(solution)/shard_map/ppermute | solution.py:292
  98.9 1.5 %collective-permute-start.25 = (bf16[544,256]{1,0:T(8,128)(2,1)S(1)}, bf16[544,256]{1,0:T(8,128)(2,1)S(1)}, u32[]{:S(2)}, u32[]{:S(2)}) collective-permute-start(bf16[544,256]{1,0:T(8,128)(2,1)S(1)} %get-tuple-element.85), channel_id=1, source_target_pairs={{0,8},{8,0},{16,24},{24,16},{1,9},{9,1},{17,25},{25,17},{2,10},{10... | collective-permute-start | bytes 835592 | tf_op jit(solution)/shard_map/ppermute | solution.py:292
  101.0 1.5 %collective-permute-start.26 = (bf16[544,256]{1,0:T(8,128)(2,1)S(1)}, bf16[544,256]{1,0:T(8,128)(2,1)S(1)}, u32[]{:S(2)}, u32[]{:S(2)}) collective-permute-start(bf16[544,256]{1,0:T(8,128)(2,1)S(1)} %get-tuple-element.86), channel_id=1, source_target_pairs={{0,16},{8,24},{16,0},{24,8},{1,17},{9,25},{17,1},{25,9},{2,18},{10... | collective-permute-start | bytes 835592 | tf_op jit(solution)/shard_map/ppermute | solution.py:292
  103.2 2.5 %collective-permute-start.27 = (bf16[544,256]{1,0:T(8,128)(2,1)S(1)}, bf16[544,256]{1,0:T(8,128)(2,1)S(1)}, u32[]{:S(2)}, u32[]{:S(2)}) collective-permute-start(bf16[544,256]{1,0:T(8,128)(2,1)S(1)} %get-tuple-element.87), channel_id=1, source_target_pairs={{0,24},{8,16},{16,8},{24,0},{1,25},{9,17},{17,9},{25,1},{2,26},{10... | collective-permute-start | bytes 835592 | tf_op jit(solution)/shard_map/ppermute | solution.py:292
  105.7 3.3 %collective-permute-done.23.refs_2_ = bf16[512,256]{1,0:T(8,128)(2,1)S(1)} collective-permute-done((bf16[512,256]{1,0:T(8,128)(2,1)S(1)}, bf16[512,256]{1,0:T(8,128)(2,1)S(1)}, u32[]{:S(2)}, u32[]{:S(2)}) %collective-permute-start.23) | collective-permute-done | bytes 262176 | tf_op jit(solution)/shard_map/ppermute | solution.py:292
  109.5 2.9 %shard_map.73 = (f32[8,128]{1,0:T(8,128)S(1)}, f32[512,256]{1,0:T(8,128)S(1)}, bf16[544,256]{1,0:T(8,128)(2,1)S(1)}, bf16[544,256]{1,0:T(8,128)(2,1)S(1)}, bf16[544,256]{1,0:T(8,128)(2,1)S(1)}) custom-call(f32[8,128]{1,0:T(8,128)S(1)} %get-tuple-element.81.token_ref, bf16[2048,2048]{1,0:T(8,128)(2,1)S(1)} %get-tuple-element.57.dense_ref, ...), custom_call_target="tpu_custom_call" | custom-call | tf_op jit(solution)/shard_map/pallas_call | solution.py:175
  113.3 1.5 %collective-permute-start.29 = (bf16[544,256]{1,0:T(8,128)(2,1)S(1)}, bf16[544,256]{1,0:T(8,128)(2,1)S(1)}, u32[]{:S(2)}, u32[]{:S(2)}) collective-permute-start(bf16[544,256]{1,0:T(8,128)(2,1)S(1)} %get-tuple-element.92), channel_id=1, source_target_pairs={{0,16},{8,24},{16,0},{24,8},{1,17},{9,25},{17,1},{25,9},{2,18},{10... | collective-permute-start | bytes 835592 | tf_op jit(solution)/shard_map/ppermute | solution.py:292
  116.9 2.2 %collective-permute-done.28.refs_0_ = bf16[544,256]{1,0:T(8,128)(2,1)S(1)} collective-permute-done((bf16[544,256]{1,0:T(8,128)(2,1)S(1)}, bf16[544,256]{1,0:T(8,128)(2,1)S(1)}, u32[]{:S(2)}, u32[]{:S(2)}) %collective-permute-start.28) | collective-permute-done | bytes 278560 | tf_op jit(solution)/shard_map/ppermute | solution.py:292
  119.1 2.8 %collective-permute-done.29.refs_1_ = bf16[544,256]{1,0:T(8,128)(2,1)S(1)} collective-permute-done((bf16[544,256]{1,0:T(8,128)(2,1)S(1)}, bf16[544,256]{1,0:T(8,128)(2,1)S(1)}, u32[]{:S(2)}, u32[]{:S(2)}) %collective-permute-start.29) | collective-permute-done | bytes 278560 | tf_op jit(solution)/shard_map/ppermute | solution.py:292
  123.9 1.5 %collective-permute-done.32 = f32[256,256]{1,0:T(8,128)S(1)} collective-permute-done((f32[256,256]{1,0:T(8,128)S(1)}, f32[256,256]{1,0:T(8,128)S(1)}, u32[]{:S(2)}, u32[]{:S(2)}) %collective-permute-start.32) | collective-permute-done | bytes 262176 | tf_op jit(solution)/shard_map/ppermute | solution.py:292
  (79 shorter events, 14.7 us)
Async XLA Ops:
  0.0 11.2 %collective-permute-start.3 = (bf16[16,256,256]{2,1,0:T(8,128)(2,1)}, bf16[16,256,256]{2,1,0:T(8,128)(2,1)}, u32[]{:S(2)}, u32[]{:S(2)}) collective-permute-start(bf16[16,256,256]{2,1,0:T(8,128)(2,1)} %bitcast.11), channel_id=1, source_target_pairs={{0,1},{1,0},{2,3},{3,2},{4,5},{5,4},{6,7},{7,6},{8,9},{9,8},{10,11... | collective-permute-start | bytes 6291464 | tf_op jit(solution)/shard_map/ppermute | solution.py:292
  2.6 2.9 %collective-permute-start = (f32[256,256]{1,0:T(8,128)}, f32[256,256]{1,0:T(8,128)S(1)}, u32[]{:S(2)}, u32[]{:S(2)}) collective-permute-start(f32[256,256]{1,0:T(8,128)} %get-tuple-element.98), channel_id=1, source_target_pairs={{0,1},{1,0},{2,3},{3,2},{4,5},{5,4},{6,7},{7,6},{8,9},{9,8},{10,11... | collective-permute-start | bytes 786440 | tf_op jit(solution)/shard_map/ppermute | solution.py:292
  4.1 20.5 %collective-permute-start.1 = (f32[256,256]{1,0:T(8,128)S(1)}, f32[256,256]{1,0:T(8,128)S(1)}, u32[]{:S(2)}, u32[]{:S(2)}) collective-permute-start(f32[256,256]{1,0:T(8,128)S(1)} %get-tuple-element.97), channel_id=1, source_target_pairs={{0,1},{1,0},{2,3},{3,2},{4,5},{5,4},{6,7},{7,6},{8,9},{9,8},{10,11... | collective-permute-start | bytes 786440 | tf_op jit(solution)/shard_map/ppermute | solution.py:292
  5.5 26.0 %collective-permute-start.9 = (bf16[512,256]{1,0:T(8,128)(2,1)S(1)}, bf16[512,256]{1,0:T(8,128)(2,1)S(1)}, u32[]{:S(2)}, u32[]{:S(2)}) collective-permute-start(bf16[512,256]{1,0:T(8,128)(2,1)S(1)} %get-tuple-element.59.refs_0_), channel_id=1, source_target_pairs={{0,6},{1,7},{2,4},{3,5},{4,2},{5,3},{6,0},{7,1},{8,14},{9,15},{10,... | collective-permute-start | bytes 786440 | tf_op jit(solution)/shard_map/ppermute | solution.py:292
  10.5 22.6 %collective-permute-start.8 = (bf16[512,256]{1,0:T(8,128)(2,1)S(1)}, bf16[512,256]{1,0:T(8,128)(2,1)S(1)}, u32[]{:S(2)}, u32[]{:S(2)}) collective-permute-start(bf16[512,256]{1,0:T(8,128)(2,1)S(1)} %get-tuple-element.59.refs_0_), channel_id=1, source_target_pairs={{0,4},{1,5},{2,6},{3,7},{4,0},{5,1},{6,2},{7,3},{8,12},{9,13},{10,... | collective-permute-start | bytes 786440 | tf_op jit(solution)/shard_map/ppermute | solution.py:292
  10.5 22.6 %collective-permute-start.7 = (bf16[512,256]{1,0:T(8,128)(2,1)S(1)}, bf16[512,256]{1,0:T(8,128)(2,1)S(1)}, u32[]{:S(2)}, u32[]{:S(2)}) collective-permute-start(bf16[512,256]{1,0:T(8,128)(2,1)S(1)} %get-tuple-element.59.refs_0_), channel_id=1, source_target_pairs={{0,2},{1,3},{2,0},{3,1},{4,6},{5,7},{6,4},{7,5},{8,10},{9,11},{10,... | collective-permute-start | bytes 786440 | tf_op jit(solution)/shard_map/ppermute | solution.py:292
  22.9 3.7 %collective-permute-start.4 = (f32[8,128]{1,0:T(8,128)S(1)}, f32[8,128]{1,0:T(8,128)S(1)}, u32[]{:S(2)}, u32[]{:S(2)}) collective-permute-start(f32[8,128]{1,0:T(8,128)S(1)} %get-tuple-element.53), channel_id=1, source_target_pairs={{0,8},{8,0},{16,24},{24,16},{1,9},{9,1},{17,25},{25,17},{2,10},{10... | collective-permute-start | bytes 12296 | tf_op jit(solution)/shard_map/ppermute | solution.py:292
  24.6 4.6 %collective-permute-start.5 = (f32[8,128]{1,0:T(8,128)S(1)}, f32[8,128]{1,0:T(8,128)S(1)}, u32[]{:S(2)}, u32[]{:S(2)}) collective-permute-start(f32[8,128]{1,0:T(8,128)S(1)} %get-tuple-element.54), channel_id=1, source_target_pairs={{0,16},{8,24},{16,0},{24,8},{1,17},{9,25},{17,1},{25,9},{2,18},{10... | collective-permute-start | bytes 12296 | tf_op jit(solution)/shard_map/ppermute | solution.py:292
  26.6 4.5 %collective-permute-start.6 = (f32[8,128]{1,0:T(8,128)S(1)}, f32[8,128]{1,0:T(8,128)S(1)}, u32[]{:S(2)}, u32[]{:S(2)}) collective-permute-start(f32[8,128]{1,0:T(8,128)S(1)} %get-tuple-element.55), channel_id=1, source_target_pairs={{0,24},{8,16},{16,8},{24,0},{1,25},{9,17},{17,9},{25,1},{2,26},{10... | collective-permute-start | bytes 12296 | tf_op jit(solution)/shard_map/ppermute | solution.py:292
  36.1 9.7 %collective-permute-start.10 = (bf16[544,256]{1,0:T(8,128)(2,1)S(1)}, bf16[544,256]{1,0:T(8,128)(2,1)S(1)}, u32[]{:S(2)}, u32[]{:S(2)}) collective-permute-start(bf16[544,256]{1,0:T(8,128)(2,1)S(1)} %get-tuple-element.65), channel_id=1, source_target_pairs={{0,8},{8,0},{16,24},{24,16},{1,9},{9,1},{17,25},{25,17},{2,10},{10... | collective-permute-start | bytes 835592 | tf_op jit(solution)/shard_map/ppermute | solution.py:292
  37.6 13.6 %collective-permute-start.11 = (bf16[544,256]{1,0:T(8,128)(2,1)S(1)}, bf16[544,256]{1,0:T(8,128)(2,1)S(1)}, u32[]{:S(2)}, u32[]{:S(2)}) collective-permute-start(bf16[544,256]{1,0:T(8,128)(2,1)S(1)} %get-tuple-element.66), channel_id=1, source_target_pairs={{0,16},{8,24},{16,0},{24,8},{1,17},{9,25},{17,1},{25,9},{2,18},{10... | collective-permute-start | bytes 835592 | tf_op jit(solution)/shard_map/ppermute | solution.py:292
  39.1 12.1 %collective-permute-start.12 = (bf16[544,256]{1,0:T(8,128)(2,1)S(1)}, bf16[544,256]{1,0:T(8,128)(2,1)S(1)}, u32[]{:S(2)}, u32[]{:S(2)}) collective-permute-start(bf16[544,256]{1,0:T(8,128)(2,1)S(1)} %get-tuple-element.67), channel_id=1, source_target_pairs={{0,24},{8,16},{16,8},{24,0},{1,25},{9,17},{17,9},{25,1},{2,26},{10... | collective-permute-start | bytes 835592 | tf_op jit(solution)/shard_map/ppermute | solution.py:292
  39.6 14.9 %collective-permute-start.15 = (bf16[512,256]{1,0:T(8,128)(2,1)S(1)}, bf16[512,256]{1,0:T(8,128)(2,1)S(1)}, u32[]{:S(2)}, u32[]{:S(2)}) collective-permute-start(bf16[512,256]{1,0:T(8,128)(2,1)S(1)} %get-tuple-element.72.refs_0_), channel_id=1, source_target_pairs={{0,6},{1,7},{2,4},{3,5},{4,2},{5,3},{6,0},{7,1},{8,14},{9,15},{10,... | collective-permute-start | bytes 786440 | tf_op jit(solution)/shard_map/ppermute | solution.py:292
  42.1 28.5 %collective-permute-start.14 = (bf16[512,256]{1,0:T(8,128)(2,1)S(1)}, bf16[512,256]{1,0:T(8,128)(2,1)S(1)}, u32[]{:S(2)}, u32[]{:S(2)}) collective-permute-start(bf16[512,256]{1,0:T(8,128)(2,1)S(1)} %get-tuple-element.72.refs_0_), channel_id=1, source_target_pairs={{0,4},{1,5},{2,6},{3,7},{4,0},{5,1},{6,2},{7,3},{8,12},{9,13},{10,... | collective-permute-start | bytes 786440 | tf_op jit(solution)/shard_map/ppermute | solution.py:292
  45.7 24.8 %collective-permute-start.13 = (bf16[512,256]{1,0:T(8,128)(2,1)S(1)}, bf16[512,256]{1,0:T(8,128)(2,1)S(1)}, u32[]{:S(2)}, u32[]{:S(2)}) collective-permute-start(bf16[512,256]{1,0:T(8,128)(2,1)S(1)} %get-tuple-element.72.refs_0_), channel_id=1, source_target_pairs={{0,2},{1,3},{2,0},{3,1},{4,6},{5,7},{6,4},{7,5},{8,10},{9,11},{10,... | collective-permute-start | bytes 786440 | tf_op jit(solution)/shard_map/ppermute | solution.py:292
  51.9 25.1 %collective-permute-start.18 = (bf16[512,256]{1,0:T(8,128)(2,1)S(1)}, bf16[512,256]{1,0:T(8,128)(2,1)S(1)}, u32[]{:S(2)}, u32[]{:S(2)}) collective-permute-start(bf16[512,256]{1,0:T(8,128)(2,1)S(1)} %get-tuple-element.74.refs_0_), channel_id=1, source_target_pairs={{0,6},{1,7},{2,4},{3,5},{4,2},{5,3},{6,0},{7,1},{8,14},{9,15},{10,... | collective-permute-start | bytes 786440 | tf_op jit(solution)/shard_map/ppermute | solution.py:292
  73.5 16.4 %collective-permute-start.19 = (bf16[544,256]{1,0:T(8,128)(2,1)S(1)}, bf16[544,256]{1,0:T(8,128)(2,1)S(1)}, u32[]{:S(2)}, u32[]{:S(2)}) collective-permute-start(bf16[544,256]{1,0:T(8,128)(2,1)S(1)} %get-tuple-element.78), channel_id=1, source_target_pairs={{0,8},{8,0},{16,24},{24,16},{1,9},{9,1},{17,25},{25,17},{2,10},{10... | collective-permute-start | bytes 835592 | tf_op jit(solution)/shard_map/ppermute | solution.py:292
  75.1 14.9 %collective-permute-start.20 = (bf16[544,256]{1,0:T(8,128)(2,1)S(1)}, bf16[544,256]{1,0:T(8,128)(2,1)S(1)}, u32[]{:S(2)}, u32[]{:S(2)}) collective-permute-start(bf16[544,256]{1,0:T(8,128)(2,1)S(1)} %get-tuple-element.79), channel_id=1, source_target_pairs={{0,16},{8,24},{16,0},{24,8},{1,17},{9,25},{17,1},{25,9},{2,18},{10... | collective-permute-start | bytes 835592 | tf_op jit(solution)/shard_map/ppermute | solution.py:292
  76.6 13.4 %collective-permute-start.21 = (bf16[544,256]{1,0:T(8,128)(2,1)S(1)}, bf16[544,256]{1,0:T(8,128)(2,1)S(1)}, u32[]{:S(2)}, u32[]{:S(2)}) collective-permute-start(bf16[544,256]{1,0:T(8,128)(2,1)S(1)} %get-tuple-element.80), channel_id=1, source_target_pairs={{0,24},{8,16},{16,8},{24,0},{1,25},{9,17},{17,9},{25,1},{2,26},{10... | collective-permute-start | bytes 835592 | tf_op jit(solution)/shard_map/ppermute | solution.py:292
  77.1 9.9 %collective-permute-start.17 = (bf16[512,256]{1,0:T(8,128)(2,1)S(1)}, bf16[512,256]{1,0:T(8,128)(2,1)S(1)}, u32[]{:S(2)}, u32[]{:S(2)}) collective-permute-start(bf16[512,256]{1,0:T(8,128)(2,1)S(1)} %get-tuple-element.74.refs_0_), channel_id=1, source_target_pairs={{0,4},{1,5},{2,6},{3,7},{4,0},{5,1},{6,2},{7,3},{8,12},{9,13},{10,... | collective-permute-start | bytes 786440 | tf_op jit(solution)/shard_map/ppermute | solution.py:292
  77.1 9.9 %collective-permute-start.16 = (bf16[512,256]{1,0:T(8,128)(2,1)S(1)}, bf16[512,256]{1,0:T(8,128)(2,1)S(1)}, u32[]{:S(2)}, u32[]{:S(2)}) collective-permute-start(bf16[512,256]{1,0:T(8,128)(2,1)S(1)} %get-tuple-element.74.refs_0_), channel_id=1, source_target_pairs={{0,2},{1,3},{2,0},{3,1},{4,6},{5,7},{6,4},{7,5},{8,10},{9,11},{10,... | collective-permute-start | bytes 786440 | tf_op jit(solution)/shard_map/ppermute | solution.py:292
  90.7 12.5 %collective-permute-start.24 = (bf16[512,256]{1,0:T(8,128)(2,1)S(1)}, bf16[512,256]{1,0:T(8,128)(2,1)S(1)}, u32[]{:S(2)}, u32[]{:S(2)}) collective-permute-start(bf16[512,256]{1,0:T(8,128)(2,1)S(1)} %get-tuple-element.82.refs_0_), channel_id=1, source_target_pairs={{0,6},{1,7},{2,4},{3,5},{4,2},{5,3},{6,0},{7,1},{8,14},{9,15},{10,... | collective-permute-start | bytes 786440 | tf_op jit(solution)/shard_map/ppermute | solution.py:292
  98.9 16.0 %collective-permute-start.25 = (bf16[544,256]{1,0:T(8,128)(2,1)S(1)}, bf16[544,256]{1,0:T(8,128)(2,1)S(1)}, u32[]{:S(2)}, u32[]{:S(2)}) collective-permute-start(bf16[544,256]{1,0:T(8,128)(2,1)S(1)} %get-tuple-element.85), channel_id=1, source_target_pairs={{0,8},{8,0},{16,24},{24,16},{1,9},{9,1},{17,25},{25,17},{2,10},{10... | collective-permute-start | bytes 835592 | tf_op jit(solution)/shard_map/ppermute | solution.py:292
  100.3 8.6 %collective-permute-start.23 = (bf16[512,256]{1,0:T(8,128)(2,1)S(1)}, bf16[512,256]{1,0:T(8,128)(2,1)S(1)}, u32[]{:S(2)}, u32[]{:S(2)}) collective-permute-start(bf16[512,256]{1,0:T(8,128)(2,1)S(1)} %get-tuple-element.82.refs_0_), channel_id=1, source_target_pairs={{0,4},{1,5},{2,6},{3,7},{4,0},{5,1},{6,2},{7,3},{8,12},{9,13},{10,... | collective-permute-start | bytes 786440 | tf_op jit(solution)/shard_map/ppermute | solution.py:292
  100.4 9.2 %collective-permute-start.22 = (bf16[512,256]{1,0:T(8,128)(2,1)S(1)}, bf16[512,256]{1,0:T(8,128)(2,1)S(1)}, u32[]{:S(2)}, u32[]{:S(2)}) collective-permute-start(bf16[512,256]{1,0:T(8,128)(2,1)S(1)} %get-tuple-element.82.refs_0_), channel_id=1, source_target_pairs={{0,2},{1,3},{2,0},{3,1},{4,6},{5,7},{6,4},{7,5},{8,10},{9,11},{10,... | collective-permute-start | bytes 786440 | tf_op jit(solution)/shard_map/ppermute | solution.py:292
  101.0 15.0 %collective-permute-start.26 = (bf16[544,256]{1,0:T(8,128)(2,1)S(1)}, bf16[544,256]{1,0:T(8,128)(2,1)S(1)}, u32[]{:S(2)}, u32[]{:S(2)}) collective-permute-start(bf16[544,256]{1,0:T(8,128)(2,1)S(1)} %get-tuple-element.86), channel_id=1, source_target_pairs={{0,16},{8,24},{16,0},{24,8},{1,17},{9,25},{17,1},{25,9},{2,18},{10... | collective-permute-start | bytes 835592 | tf_op jit(solution)/shard_map/ppermute | solution.py:292
  103.2 12.8 %collective-permute-start.27 = (bf16[544,256]{1,0:T(8,128)(2,1)S(1)}, bf16[544,256]{1,0:T(8,128)(2,1)S(1)}, u32[]{:S(2)}, u32[]{:S(2)}) collective-permute-start(bf16[544,256]{1,0:T(8,128)(2,1)S(1)} %get-tuple-element.87), channel_id=1, source_target_pairs={{0,24},{8,16},{16,8},{24,0},{1,25},{9,17},{17,9},{25,1},{2,26},{10... | collective-permute-start | bytes 835592 | tf_op jit(solution)/shard_map/ppermute | solution.py:292
  112.5 6.6 %collective-permute-start.28 = (bf16[544,256]{1,0:T(8,128)(2,1)S(1)}, bf16[544,256]{1,0:T(8,128)(2,1)S(1)}, u32[]{:S(2)}, u32[]{:S(2)}) collective-permute-start(bf16[544,256]{1,0:T(8,128)(2,1)S(1)} %get-tuple-element.91), channel_id=1, source_target_pairs={{0,8},{8,0},{16,24},{24,16},{1,9},{9,1},{17,25},{25,17},{2,10},{10... | collective-permute-start | bytes 835592 | tf_op jit(solution)/shard_map/ppermute | solution.py:292
  113.3 8.6 %collective-permute-start.29 = (bf16[544,256]{1,0:T(8,128)(2,1)S(1)}, bf16[544,256]{1,0:T(8,128)(2,1)S(1)}, u32[]{:S(2)}, u32[]{:S(2)}) collective-permute-start(bf16[544,256]{1,0:T(8,128)(2,1)S(1)} %get-tuple-element.92), channel_id=1, source_target_pairs={{0,16},{8,24},{16,0},{24,8},{1,17},{9,25},{17,1},{25,9},{2,18},{10... | collective-permute-start | bytes 835592 | tf_op jit(solution)/shard_map/ppermute | solution.py:292
  114.8 8.2 %collective-permute-start.30 = (bf16[544,256]{1,0:T(8,128)(2,1)S(1)}, bf16[544,256]{1,0:T(8,128)(2,1)S(1)}, u32[]{:S(2)}, u32[]{:S(2)}) collective-permute-start(bf16[544,256]{1,0:T(8,128)(2,1)S(1)} %get-tuple-element.93), channel_id=1, source_target_pairs={{0,24},{8,16},{16,8},{24,0},{1,25},{9,17},{17,9},{25,1},{2,26},{10... | collective-permute-start | bytes 835592 | tf_op jit(solution)/shard_map/ppermute | solution.py:292
  116.8 7.1 %collective-permute-start.31 = (f32[256,256]{1,0:T(8,128)S(1)}, f32[256,256]{1,0:T(8,128)S(1)}, u32[]{:S(2)}, u32[]{:S(2)}) collective-permute-start(f32[256,256]{1,0:T(8,128)S(1)} %get-tuple-element.102), channel_id=1, source_target_pairs={{0,1},{1,0},{2,3},{3,2},{4,5},{5,4},{6,7},{7,6},{8,9},{9,8},{10,11... | collective-permute-start | bytes 786440 | tf_op jit(solution)/shard_map/ppermute | solution.py:292
  123.8 1.6 %collective-permute-start.32 = (f32[256,256]{1,0:T(8,128)S(1)}, f32[256,256]{1,0:T(8,128)S(1)}, u32[]{:S(2)}, u32[]{:S(2)}) collective-permute-start(f32[256,256]{1,0:T(8,128)S(1)} %get-tuple-element.104), channel_id=1, source_target_pairs={{0,1},{1,0},{2,3},{3,2},{4,5},{5,4},{6,7},{7,6},{8,9},{9,8},{10,11... | collective-permute-start | bytes 786440 | tf_op jit(solution)/shard_map/ppermute | solution.py:292
  (5 other events, 22.8 us)

commit v3 on v2

--- a/solution.py
+++ b/solution.py
@@ -308,6 +308,7 @@
     for s, w in zip(starts, widths):
         kept = lax.dynamic_slice_in_dim(labels, core * half + s, w, 1)
         given = lax.dynamic_slice_in_dim(labels, (1 - core) * half + s, w, 1)
+        kept, given = lax.optimization_barrier((kept, given))
         halves.append((kept, swap(given, "col", 1)))
 
     live = jnp.arange(slots) < block_count[0, 0]

time: 127 us -> 127 us (level)
  no operation moved by 1% of the time
where the time goes in v3:
time: 127 us
  waiting for transfers between devices  49.3 us (39%)
  starting transfers between devices  45.3 us (36%)
  Pallas kernels  26.8 us (21%)
  local copies, waits for them, and re-layouts  2.69 us (2%)
  other arithmetic  1.54 us (1%)
    ppermute x33, waiting for transfers between devices, swap(): return lax.ppermute(x, axis, [(i, i ^ mask) for i in range(size)])  49.3 us
    ppermute x33, starting transfers between devices, swap(): return lax.ppermute(x, axis, [(i, i ^ mask) for i in range(size)])  45.3 us
    pallas_call x4, Pallas kernels, terms(): pl.pallas_call(functools.partial(term_kernel if whole else term_step_kern...  11.7 us
    pallas_call x1, Pallas kernels, dense_tiles(): pl.pallas_call(dense_kernel, out_shape=[dense, jax.ShapeDtypeStruct((2 *...  11.7 us
    pallas_call x4, Pallas kernels, update(): pl.pallas_call(functools.partial(update_kernel, len(codes)), out_shape=[j...  2.85 us
  transfers between devices with their start and end apart: 33, of which 15 were waited for; matrix products, arithmetic and copies ran while one was open for 2% of the time, Pallas kernels for 18%

profile of v3, /device:TPU:0, one launch (start us, length us, event | category | flops | bytes accessed | tf_op | source)
XLA Modules:
  0.0 126.6 jit_solution(14079657059405867505)
XLA Ops:
  0.5 2.0 %constant_dynamic-slice_fusion = (f32[256,256]{1,0:T(8,128)S(1)}, f32[256,256]{1,0:T(8,128)}, f32[256,256]{1,0:T(8,128)S(1)}, f32[256,256]{1,0:T(8,128)S(1)}) fusion(f32[256,1024]{1,0:T(8,128)} %param.10, s32[]{:T(128)S(6)} %select_n.32, s32[]{:T(128)S(6)} %select_n.30, s32[]{:T(128)S(6)} %select_n.29, s32[]{:T(128)S(6)} %select_n.31), kind=kLoop, calls=%fused_computation.14 | loop fusion | bytes 2097168 | tf_op jit(solution)/shard_map/dynamic_slice | solution.py:310
  5.5 5.0 %collective-permute-start.9 = (bf16[512,256]{1,0:T(8,128)(2,1)S(1)}, bf16[512,256]{1,0:T(8,128)(2,1)S(1)}, u32[]{:S(2)}, u32[]{:S(2)}) collective-permute-start(bf16[512,256]{1,0:T(8,128)(2,1)S(1)} %get-tuple-element.67.refs_0_), channel_id=1, source_target_pairs={{0,6},{1,7},{2,4},{3,5},{4,2},{5,3},{6,0},{7,1},{8,14},{9,15},{10,... | collective-permute-start | bytes 786440 | tf_op jit(solution)/shard_map/ppermute | solution.py:292
  11.2 11.7 %shard_map.66 = (bf16[2048,2048]{1,0:T(8,128)(2,1)S(1)}, f32[2048,128]{1,0:T(8,128)S(1)}, f32[8,128]{1,0:T(8,128)S(1)}, f32[8,128]{1,0:T(8,128)S(1)}, f32[8,128]{1,0:T(8,128)S(1)}, /*index=5*/f32[8,128]{1,0:T(8,128)S(1)}) custom-call(s32[4,16]{1,0:T(4,128)S(1)} %pad_add_fusion.1.slot_ref, bf16[16,256,256]{2,1,0:T(8,128)(2,1)S(1)} %bitcast.12, ...), custom_call_target="tpu_custom_call" | custom-call | tf_op jit(solution)/shard_map/pallas_call | solution.py:67
  22.9 1.7 %collective-permute-start.4 = (f32[8,128]{1,0:T(8,128)S(1)}, f32[8,128]{1,0:T(8,128)S(1)}, u32[]{:S(2)}, u32[]{:S(2)}) collective-permute-start(f32[8,128]{1,0:T(8,128)S(1)} %get-tuple-element.61), channel_id=1, source_target_pairs={{0,8},{8,0},{16,24},{24,16},{1,9},{9,1},{17,25},{25,17},{2,10},{10... | collective-permute-start | bytes 12296 | tf_op jit(solution)/shard_map/ppermute | solution.py:292
  24.6 1.6 %collective-permute-start.5 = (f32[8,128]{1,0:T(8,128)S(1)}, f32[8,128]{1,0:T(8,128)S(1)}, u32[]{:S(2)}, u32[]{:S(2)}) collective-permute-start(f32[8,128]{1,0:T(8,128)S(1)} %get-tuple-element.62), channel_id=1, source_target_pairs={{0,16},{8,24},{16,0},{24,8},{1,17},{9,25},{17,1},{25,9},{2,18},{10... | collective-permute-start | bytes 12296 | tf_op jit(solution)/shard_map/ppermute | solution.py:292
  26.6 2.6 %collective-permute-start.6 = (f32[8,128]{1,0:T(8,128)S(1)}, f32[8,128]{1,0:T(8,128)S(1)}, u32[]{:S(2)}, u32[]{:S(2)}) collective-permute-start(f32[8,128]{1,0:T(8,128)S(1)} %get-tuple-element.63), channel_id=1, source_target_pairs={{0,24},{8,16},{16,8},{24,0},{1,25},{9,17},{17,9},{25,1},{2,26},{10... | collective-permute-start | bytes 12296 | tf_op jit(solution)/shard_map/ppermute | solution.py:292
  29.2 1.8 %collective-permute-done.6.refs_3_ = f32[8,128]{1,0:T(8,128)S(1)} collective-permute-done((f32[8,128]{1,0:T(8,128)S(1)}, f32[8,128]{1,0:T(8,128)S(1)}, u32[]{:S(2)}, u32[]{:S(2)}) %collective-permute-start.6) | collective-permute-done | bytes 4128 | tf_op jit(solution)/shard_map/ppermute | solution.py:292
  31.5 1.6 %collective-permute-done.8.refs_2_ = bf16[512,256]{1,0:T(8,128)(2,1)S(1)} collective-permute-done((bf16[512,256]{1,0:T(8,128)(2,1)S(1)}, bf16[512,256]{1,0:T(8,128)(2,1)S(1)}, u32[]{:S(2)}, u32[]{:S(2)}) %collective-permute-start.8) | collective-permute-done | bytes 262176 | tf_op jit(solution)/shard_map/ppermute | solution.py:292
  33.1 2.9 %shard_map.68 = (f32[8,128]{1,0:T(8,128)S(1)}, f32[512,256]{1,0:T(8,128)S(1)}, bf16[544,256]{1,0:T(8,128)(2,1)S(1)}, bf16[544,256]{1,0:T(8,128)(2,1)S(1)}, bf16[544,256]{1,0:T(8,128)(2,1)S(1)}) custom-call(f32[8,128]{1,0:T(8,128)S(1)} %get-tuple-element.64.token_ref, bf16[2048,2048]{1,0:T(8,128)(2,1)S(1)} %get-tuple-element.65.dense_ref, ...), custom_call_target="tpu_custom_call" | custom-call | tf_op jit(solution)/shard_map/pallas_call | solution.py:175
  36.1 1.6 %collective-permute-start.10 = (bf16[544,256]{1,0:T(8,128)(2,1)S(1)}, bf16[544,256]{1,0:T(8,128)(2,1)S(1)}, u32[]{:S(2)}, u32[]{:S(2)}) collective-permute-start(bf16[544,256]{1,0:T(8,128)(2,1)S(1)} %get-tuple-element.73), channel_id=1, source_target_pairs={{0,8},{8,0},{16,24},{24,16},{1,9},{9,1},{17,25},{25,17},{2,10},{10... | collective-permute-start | bytes 835592 | tf_op jit(solution)/shard_map/ppermute | solution.py:292
  37.6 1.5 %collective-permute-start.11 = (bf16[544,256]{1,0:T(8,128)(2,1)S(1)}, bf16[544,256]{1,0:T(8,128)(2,1)S(1)}, u32[]{:S(2)}, u32[]{:S(2)}) collective-permute-start(bf16[544,256]{1,0:T(8,128)(2,1)S(1)} %get-tuple-element.74), channel_id=1, source_target_pairs={{0,16},{8,24},{16,0},{24,8},{1,17},{9,25},{17,1},{25,9},{2,18},{10... | collective-permute-start | bytes 835592 | tf_op jit(solution)/shard_map/ppermute | solution.py:292
  39.6 2.5 %collective-permute-start.15 = (bf16[512,256]{1,0:T(8,128)(2,1)S(1)}, bf16[512,256]{1,0:T(8,128)(2,1)S(1)}, u32[]{:S(2)}, u32[]{:S(2)}) collective-permute-start(bf16[512,256]{1,0:T(8,128)(2,1)S(1)} %get-tuple-element.80.refs_0_), channel_id=1, source_target_pairs={{0,6},{1,7},{2,4},{3,5},{4,2},{5,3},{6,0},{7,1},{8,14},{9,15},{10,... | collective-permute-start | bytes 786440 | tf_op jit(solution)/shard_map/ppermute | solution.py:292
  42.1 3.6 %collective-permute-done.10.refs_0_ = bf16[544,256]{1,0:T(8,128)(2,1)S(1)} collective-permute-done((bf16[544,256]{1,0:T(8,128)(2,1)S(1)}, bf16[544,256]{1,0:T(8,128)(2,1)S(1)}, u32[]{:S(2)}, u32[]{:S(2)}) %collective-permute-start.10) | collective-permute-done | bytes 278560 | tf_op jit(solution)/shard_map/ppermute | solution.py:292
  45.7 5.5 %collective-permute-done.11.refs_1_ = bf16[544,256]{1,0:T(8,128)(2,1)S(1)} collective-permute-done((bf16[544,256]{1,0:T(8,128)(2,1)S(1)}, bf16[544,256]{1,0:T(8,128)(2,1)S(1)}, u32[]{:S(2)}, u32[]{:S(2)}) %collective-permute-start.11) | collective-permute-done | bytes 278560 | tf_op jit(solution)/shard_map/ppermute | solution.py:292
  51.9 2.5 %collective-permute-start.18 = (bf16[512,256]{1,0:T(8,128)(2,1)S(1)}, bf16[512,256]{1,0:T(8,128)(2,1)S(1)}, u32[]{:S(2)}, u32[]{:S(2)}) collective-permute-start(bf16[512,256]{1,0:T(8,128)(2,1)S(1)} %get-tuple-element.82.refs_0_), channel_id=1, source_target_pairs={{0,6},{1,7},{2,4},{3,5},{4,2},{5,3},{6,0},{7,1},{8,14},{9,15},{10,... | collective-permute-start | bytes 786440 | tf_op jit(solution)/shard_map/ppermute | solution.py:292
  54.5 16.1 %collective-permute-done.14.refs_2_ = bf16[512,256]{1,0:T(8,128)(2,1)S(1)} collective-permute-done((bf16[512,256]{1,0:T(8,128)(2,1)S(1)}, bf16[512,256]{1,0:T(8,128)(2,1)S(1)}, u32[]{:S(2)}, u32[]{:S(2)}) %collective-permute-start.14) | collective-permute-done | bytes 262176 | tf_op jit(solution)/shard_map/ppermute | solution.py:292
  70.6 2.9 %shard_map.70 = (f32[8,128]{1,0:T(8,128)S(1)}, f32[512,256]{1,0:T(8,128)S(1)}, bf16[544,256]{1,0:T(8,128)(2,1)S(1)}, bf16[544,256]{1,0:T(8,128)(2,1)S(1)}, bf16[544,256]{1,0:T(8,128)(2,1)S(1)}) custom-call(f32[8,128]{1,0:T(8,128)S(1)} %get-tuple-element.79.token_ref, bf16[2048,2048]{1,0:T(8,128)(2,1)S(1)} %get-tuple-element.65.dense_ref, ...), custom_call_target="tpu_custom_call" | custom-call | tf_op jit(solution)/shard_map/pallas_call | solution.py:175
  73.5 1.6 %collective-permute-start.19 = (bf16[544,256]{1,0:T(8,128)(2,1)S(1)}, bf16[544,256]{1,0:T(8,128)(2,1)S(1)}, u32[]{:S(2)}, u32[]{:S(2)}) collective-permute-start(bf16[544,256]{1,0:T(8,128)(2,1)S(1)} %get-tuple-element.86), channel_id=1, source_target_pairs={{0,8},{8,0},{16,24},{24,16},{1,9},{9,1},{17,25},{25,17},{2,10},{10... | collective-permute-start | bytes 835592 | tf_op jit(solution)/shard_map/ppermute | solution.py:292
  75.1 1.5 %collective-permute-start.20 = (bf16[544,256]{1,0:T(8,128)(2,1)S(1)}, bf16[544,256]{1,0:T(8,128)(2,1)S(1)}, u32[]{:S(2)}, u32[]{:S(2)}) collective-permute-start(bf16[544,256]{1,0:T(8,128)(2,1)S(1)} %get-tuple-element.87), channel_id=1, source_target_pairs={{0,16},{8,24},{16,0},{24,8},{1,17},{9,25},{17,1},{25,9},{2,18},{10... | collective-permute-start | bytes 835592 | tf_op jit(solution)/shard_map/ppermute | solution.py:292
  77.1 2.5 %collective-permute-start.16 = (bf16[512,256]{1,0:T(8,128)(2,1)S(1)}, bf16[512,256]{1,0:T(8,128)(2,1)S(1)}, u32[]{:S(2)}, u32[]{:S(2)}) collective-permute-start(bf16[512,256]{1,0:T(8,128)(2,1)S(1)} %get-tuple-element.82.refs_0_), channel_id=1, source_target_pairs={{0,2},{1,3},{2,0},{3,1},{4,6},{5,7},{6,4},{7,5},{8,10},{9,11},{10,... | collective-permute-start | bytes 786440 | tf_op jit(solution)/shard_map/ppermute | solution.py:292
  79.6 7.4 %collective-permute-done.17.refs_2_ = bf16[512,256]{1,0:T(8,128)(2,1)S(1)} collective-permute-done((bf16[512,256]{1,0:T(8,128)(2,1)S(1)}, bf16[512,256]{1,0:T(8,128)(2,1)S(1)}, u32[]{:S(2)}, u32[]{:S(2)}) %collective-permute-start.17) | collective-permute-done | bytes 262176 | tf_op jit(solution)/shard_map/ppermute | solution.py:292
  87.0 2.9 %shard_map.71 = (f32[8,128]{1,0:T(8,128)S(1)}, f32[512,256]{1,0:T(8,128)S(1)}, bf16[544,256]{1,0:T(8,128)(2,1)S(1)}, bf16[544,256]{1,0:T(8,128)(2,1)S(1)}, bf16[544,256]{1,0:T(8,128)(2,1)S(1)}) custom-call(f32[8,128]{1,0:T(8,128)S(1)} %get-tuple-element.81.token_ref, bf16[2048,2048]{1,0:T(8,128)(2,1)S(1)} %get-tuple-element.65.dense_ref, ...), custom_call_target="tpu_custom_call" | custom-call | tf_op jit(solution)/shard_map/pallas_call | solution.py:175
  90.7 8.2 %collective-permute-start.24 = (bf16[512,256]{1,0:T(8,128)(2,1)S(1)}, bf16[512,256]{1,0:T(8,128)(2,1)S(1)}, u32[]{:S(2)}, u32[]{:S(2)}) collective-permute-start(bf16[512,256]{1,0:T(8,128)(2,1)S(1)} %get-tuple-element.90.refs_0_), channel_id=1, source_target_pairs={{0,6},{1,7},{2,4},{3,5},{4,2},{5,3},{6,0},{7,1},{8,14},{9,15},{10,... | collective-permute-start | bytes 786440 | tf_op jit(solution)/shard_map/ppermute | solution.py:292
  98.9 1.5 %collective-permute-start.25 = (bf16[544,256]{1,0:T(8,128)(2,1)S(1)}, bf16[544,256]{1,0:T(8,128)(2,1)S(1)}, u32[]{:S(2)}, u32[]{:S(2)}) collective-permute-start(bf16[544,256]{1,0:T(8,128)(2,1)S(1)} %get-tuple-element.93), channel_id=1, source_target_pairs={{0,8},{8,0},{16,24},{24,16},{1,9},{9,1},{17,25},{25,17},{2,10},{10... | collective-permute-start | bytes 835592 | tf_op jit(solution)/shard_map/ppermute | solution.py:292
  101.0 1.5 %collective-permute-start.26 = (bf16[544,256]{1,0:T(8,128)(2,1)S(1)}, bf16[544,256]{1,0:T(8,128)(2,1)S(1)}, u32[]{:S(2)}, u32[]{:S(2)}) collective-permute-start(bf16[544,256]{1,0:T(8,128)(2,1)S(1)} %get-tuple-element.94), channel_id=1, source_target_pairs={{0,16},{8,24},{16,0},{24,8},{1,17},{9,25},{17,1},{25,9},{2,18},{10... | collective-permute-start | bytes 835592 | tf_op jit(solution)/shard_map/ppermute | solution.py:292
  103.2 2.5 %collective-permute-start.27 = (bf16[544,256]{1,0:T(8,128)(2,1)S(1)}, bf16[544,256]{1,0:T(8,128)(2,1)S(1)}, u32[]{:S(2)}, u32[]{:S(2)}) collective-permute-start(bf16[544,256]{1,0:T(8,128)(2,1)S(1)} %get-tuple-element.95), channel_id=1, source_target_pairs={{0,24},{8,16},{16,8},{24,0},{1,25},{9,17},{17,9},{25,1},{2,26},{10... | collective-permute-start | bytes 835592 | tf_op jit(solution)/shard_map/ppermute | solution.py:292
  105.7 3.3 %collective-permute-done.23.refs_2_ = bf16[512,256]{1,0:T(8,128)(2,1)S(1)} collective-permute-done((bf16[512,256]{1,0:T(8,128)(2,1)S(1)}, bf16[512,256]{1,0:T(8,128)(2,1)S(1)}, u32[]{:S(2)}, u32[]{:S(2)}) %collective-permute-start.23) | collective-permute-done | bytes 262176 | tf_op jit(solution)/shard_map/ppermute | solution.py:292
  109.5 2.9 %shard_map.73 = (f32[8,128]{1,0:T(8,128)S(1)}, f32[512,256]{1,0:T(8,128)S(1)}, bf16[544,256]{1,0:T(8,128)(2,1)S(1)}, bf16[544,256]{1,0:T(8,128)(2,1)S(1)}, bf16[544,256]{1,0:T(8,128)(2,1)S(1)}) custom-call(f32[8,128]{1,0:T(8,128)S(1)} %get-tuple-element.89.token_ref, bf16[2048,2048]{1,0:T(8,128)(2,1)S(1)} %get-tuple-element.65.dense_ref, ...), custom_call_target="tpu_custom_call" | custom-call | tf_op jit(solution)/shard_map/pallas_call | solution.py:175
  113.3 1.5 %collective-permute-start.29 = (bf16[544,256]{1,0:T(8,128)(2,1)S(1)}, bf16[544,256]{1,0:T(8,128)(2,1)S(1)}, u32[]{:S(2)}, u32[]{:S(2)}) collective-permute-start(bf16[544,256]{1,0:T(8,128)(2,1)S(1)} %get-tuple-element.100), channel_id=1, source_target_pairs={{0,16},{8,24},{16,0},{24,8},{1,17},{9,25},{17,1},{25,9},{2,18},{10... | collective-permute-start | bytes 835592 | tf_op jit(solution)/shard_map/ppermute | solution.py:292
  116.9 2.2 %collective-permute-done.28.refs_0_ = bf16[544,256]{1,0:T(8,128)(2,1)S(1)} collective-permute-done((bf16[544,256]{1,0:T(8,128)(2,1)S(1)}, bf16[544,256]{1,0:T(8,128)(2,1)S(1)}, u32[]{:S(2)}, u32[]{:S(2)}) %collective-permute-start.28) | collective-permute-done | bytes 278560 | tf_op jit(solution)/shard_map/ppermute | solution.py:292
  119.1 2.8 %collective-permute-done.29.refs_1_ = bf16[544,256]{1,0:T(8,128)(2,1)S(1)} collective-permute-done((bf16[544,256]{1,0:T(8,128)(2,1)S(1)}, bf16[544,256]{1,0:T(8,128)(2,1)S(1)}, u32[]{:S(2)}, u32[]{:S(2)}) %collective-permute-start.29) | collective-permute-done | bytes 278560 | tf_op jit(solution)/shard_map/ppermute | solution.py:292
  123.9 1.5 %collective-permute-done.32 = f32[256,256]{1,0:T(8,128)S(1)} collective-permute-done((f32[256,256]{1,0:T(8,128)S(1)}, f32[256,256]{1,0:T(8,128)S(1)}, u32[]{:S(2)}, u32[]{:S(2)}) %collective-permute-start.32) | collective-permute-done | bytes 262176 | tf_op jit(solution)/shard_map/ppermute | solution.py:292
  (79 shorter events, 14.7 us)
Async XLA Ops:
  0.0 11.2 %collective-permute-start.3 = (bf16[16,256,256]{2,1,0:T(8,128)(2,1)}, bf16[16,256,256]{2,1,0:T(8,128)(2,1)}, u32[]{:S(2)}, u32[]{:S(2)}) collective-permute-start(bf16[16,256,256]{2,1,0:T(8,128)(2,1)} %bitcast.11), channel_id=1, source_target_pairs={{0,1},{1,0},{2,3},{3,2},{4,5},{5,4},{6,7},{7,6},{8,9},{9,8},{10,11... | collective-permute-start | bytes 6291464 | tf_op jit(solution)/shard_map/ppermute | solution.py:292
  2.6 2.9 %collective-permute-start = (f32[256,256]{1,0:T(8,128)}, f32[256,256]{1,0:T(8,128)S(1)}, u32[]{:S(2)}, u32[]{:S(2)}) collective-permute-start(f32[256,256]{1,0:T(8,128)} %get-tuple-element.55), channel_id=1, source_target_pairs={{0,1},{1,0},{2,3},{3,2},{4,5},{5,4},{6,7},{7,6},{8,9},{9,8},{10,11... | collective-permute-start | bytes 786440 | tf_op jit(solution)/shard_map/ppermute | solution.py:292
  4.1 20.5 %collective-permute-start.1 = (f32[256,256]{1,0:T(8,128)S(1)}, f32[256,256]{1,0:T(8,128)S(1)}, u32[]{:S(2)}, u32[]{:S(2)}) collective-permute-start(f32[256,256]{1,0:T(8,128)S(1)} %get-tuple-element.58), channel_id=1, source_target_pairs={{0,1},{1,0},{2,3},{3,2},{4,5},{5,4},{6,7},{7,6},{8,9},{9,8},{10,11... | collective-permute-start | bytes 786440 | tf_op jit(solution)/shard_map/ppermute | solution.py:292
  5.5 26.0 %collective-permute-start.9 = (bf16[512,256]{1,0:T(8,128)(2,1)S(1)}, bf16[512,256]{1,0:T(8,128)(2,1)S(1)}, u32[]{:S(2)}, u32[]{:S(2)}) collective-permute-start(bf16[512,256]{1,0:T(8,128)(2,1)S(1)} %get-tuple-element.67.refs_0_), channel_id=1, source_target_pairs={{0,6},{1,7},{2,4},{3,5},{4,2},{5,3},{6,0},{7,1},{8,14},{9,15},{10,... | collective-permute-start | bytes 786440 | tf_op jit(solution)/shard_map/ppermute | solution.py:292
  10.5 22.6 %collective-permute-start.8 = (bf16[512,256]{1,0:T(8,128)(2,1)S(1)}, bf16[512,256]{1,0:T(8,128)(2,1)S(1)}, u32[]{:S(2)}, u32[]{:S(2)}) collective-permute-start(bf16[512,256]{1,0:T(8,128)(2,1)S(1)} %get-tuple-element.67.refs_0_), channel_id=1, source_target_pairs={{0,4},{1,5},{2,6},{3,7},{4,0},{5,1},{6,2},{7,3},{8,12},{9,13},{10,... | collective-permute-start | bytes 786440 | tf_op jit(solution)/shard_map/ppermute | solution.py:292
  10.5 22.6 %collective-permute-start.7 = (bf16[512,256]{1,0:T(8,128)(2,1)S(1)}, bf16[512,256]{1,0:T(8,128)(2,1)S(1)}, u32[]{:S(2)}, u32[]{:S(2)}) collective-permute-start(bf16[512,256]{1,0:T(8,128)(2,1)S(1)} %get-tuple-element.67.refs_0_), channel_id=1, source_target_pairs={{0,2},{1,3},{2,0},{3,1},{4,6},{5,7},{6,4},{7,5},{8,10},{9,11},{10,... | collective-permute-start | bytes 786440 | tf_op jit(solution)/shard_map/ppermute | solution.py:292
  22.9 3.7 %collective-permute-start.4 = (f32[8,128]{1,0:T(8,128)S(1)}, f32[8,128]{1,0:T(8,128)S(1)}, u32[]{:S(2)}, u32[]{:S(2)}) collective-permute-start(f32[8,128]{1,0:T(8,128)S(1)} %get-tuple-element.61), channel_id=1, source_target_pairs={{0,8},{8,0},{16,24},{24,16},{1,9},{9,1},{17,25},{25,17},{2,10},{10... | collective-permute-start | bytes 12296 | tf_op jit(solution)/shard_map/ppermute | solution.py:292
  24.6 4.6 %collective-permute-start.5 = (f32[8,128]{1,0:T(8,128)S(1)}, f32[8,128]{1,0:T(8,128)S(1)}, u32[]{:S(2)}, u32[]{:S(2)}) collective-permute-start(f32[8,128]{1,0:T(8,128)S(1)} %get-tuple-element.62), channel_id=1, source_target_pairs={{0,16},{8,24},{16,0},{24,8},{1,17},{9,25},{17,1},{25,9},{2,18},{10... | collective-permute-start | bytes 12296 | tf_op jit(solution)/shard_map/ppermute | solution.py:292
  26.6 4.5 %collective-permute-start.6 = (f32[8,128]{1,0:T(8,128)S(1)}, f32[8,128]{1,0:T(8,128)S(1)}, u32[]{:S(2)}, u32[]{:S(2)}) collective-permute-start(f32[8,128]{1,0:T(8,128)S(1)} %get-tuple-element.63), channel_id=1, source_target_pairs={{0,24},{8,16},{16,8},{24,0},{1,25},{9,17},{17,9},{25,1},{2,26},{10... | collective-permute-start | bytes 12296 | tf_op jit(solution)/shard_map/ppermute | solution.py:292
  36.1 9.7 %collective-permute-start.10 = (bf16[544,256]{1,0:T(8,128)(2,1)S(1)}, bf16[544,256]{1,0:T(8,128)(2,1)S(1)}, u32[]{:S(2)}, u32[]{:S(2)}) collective-permute-start(bf16[544,256]{1,0:T(8,128)(2,1)S(1)} %get-tuple-element.73), channel_id=1, source_target_pairs={{0,8},{8,0},{16,24},{24,16},{1,9},{9,1},{17,25},{25,17},{2,10},{10... | collective-permute-start | bytes 835592 | tf_op jit(solution)/shard_map/ppermute | solution.py:292
  37.6 13.6 %collective-permute-start.11 = (bf16[544,256]{1,0:T(8,128)(2,1)S(1)}, bf16[544,256]{1,0:T(8,128)(2,1)S(1)}, u32[]{:S(2)}, u32[]{:S(2)}) collective-permute-start(bf16[544,256]{1,0:T(8,128)(2,1)S(1)} %get-tuple-element.74), channel_id=1, source_target_pairs={{0,16},{8,24},{16,0},{24,8},{1,17},{9,25},{17,1},{25,9},{2,18},{10... | collective-permute-start | bytes 835592 | tf_op jit(solution)/shard_map/ppermute | solution.py:292
  39.1 12.1 %collective-permute-start.12 = (bf16[544,256]{1,0:T(8,128)(2,1)S(1)}, bf16[544,256]{1,0:T(8,128)(2,1)S(1)}, u32[]{:S(2)}, u32[]{:S(2)}) collective-permute-start(bf16[544,256]{1,0:T(8,128)(2,1)S(1)} %get-tuple-element.75), channel_id=1, source_target_pairs={{0,24},{8,16},{16,8},{24,0},{1,25},{9,17},{17,9},{25,1},{2,26},{10... | collective-permute-start | bytes 835592 | tf_op jit(solution)/shard_map/ppermute | solution.py:292
  39.6 14.9 %collective-permute-start.15 = (bf16[512,256]{1,0:T(8,128)(2,1)S(1)}, bf16[512,256]{1,0:T(8,128)(2,1)S(1)}, u32[]{:S(2)}, u32[]{:S(2)}) collective-permute-start(bf16[512,256]{1,0:T(8,128)(2,1)S(1)} %get-tuple-element.80.refs_0_), channel_id=1, source_target_pairs={{0,6},{1,7},{2,4},{3,5},{4,2},{5,3},{6,0},{7,1},{8,14},{9,15},{10,... | collective-permute-start | bytes 786440 | tf_op jit(solution)/shard_map/ppermute | solution.py:292
  42.1 28.5 %collective-permute-start.14 = (bf16[512,256]{1,0:T(8,128)(2,1)S(1)}, bf16[512,256]{1,0:T(8,128)(2,1)S(1)}, u32[]{:S(2)}, u32[]{:S(2)}) collective-permute-start(bf16[512,256]{1,0:T(8,128)(2,1)S(1)} %get-tuple-element.80.refs_0_), channel_id=1, source_target_pairs={{0,4},{1,5},{2,6},{3,7},{4,0},{5,1},{6,2},{7,3},{8,12},{9,13},{10,... | collective-permute-start | bytes 786440 | tf_op jit(solution)/shard_map/ppermute | solution.py:292
  45.7 24.8 %collective-permute-start.13 = (bf16[512,256]{1,0:T(8,128)(2,1)S(1)}, bf16[512,256]{1,0:T(8,128)(2,1)S(1)}, u32[]{:S(2)}, u32[]{:S(2)}) collective-permute-start(bf16[512,256]{1,0:T(8,128)(2,1)S(1)} %get-tuple-element.80.refs_0_), channel_id=1, source_target_pairs={{0,2},{1,3},{2,0},{3,1},{4,6},{5,7},{6,4},{7,5},{8,10},{9,11},{10,... | collective-permute-start | bytes 786440 | tf_op jit(solution)/shard_map/ppermute | solution.py:292
  51.9 25.1 %collective-permute-start.18 = (bf16[512,256]{1,0:T(8,128)(2,1)S(1)}, bf16[512,256]{1,0:T(8,128)(2,1)S(1)}, u32[]{:S(2)}, u32[]{:S(2)}) collective-permute-start(bf16[512,256]{1,0:T(8,128)(2,1)S(1)} %get-tuple-element.82.refs_0_), channel_id=1, source_target_pairs={{0,6},{1,7},{2,4},{3,5},{4,2},{5,3},{6,0},{7,1},{8,14},{9,15},{10,... | collective-permute-start | bytes 786440 | tf_op jit(solution)/shard_map/ppermute | solution.py:292
  73.5 16.4 %collective-permute-start.19 = (bf16[544,256]{1,0:T(8,128)(2,1)S(1)}, bf16[544,256]{1,0:T(8,128)(2,1)S(1)}, u32[]{:S(2)}, u32[]{:S(2)}) collective-permute-start(bf16[544,256]{1,0:T(8,128)(2,1)S(1)} %get-tuple-element.86), channel_id=1, source_target_pairs={{0,8},{8,0},{16,24},{24,16},{1,9},{9,1},{17,25},{25,17},{2,10},{10... | collective-permute-start | bytes 835592 | tf_op jit(solution)/shard_map/ppermute | solution.py:292
  75.1 14.9 %collective-permute-start.20 = (bf16[544,256]{1,0:T(8,128)(2,1)S(1)}, bf16[544,256]{1,0:T(8,128)(2,1)S(1)}, u32[]{:S(2)}, u32[]{:S(2)}) collective-permute-start(bf16[544,256]{1,0:T(8,128)(2,1)S(1)} %get-tuple-element.87), channel_id=1, source_target_pairs={{0,16},{8,24},{16,0},{24,8},{1,17},{9,25},{17,1},{25,9},{2,18},{10... | collective-permute-start | bytes 835592 | tf_op jit(solution)/shard_map/ppermute | solution.py:292
  76.6 13.4 %collective-permute-start.21 = (bf16[544,256]{1,0:T(8,128)(2,1)S(1)}, bf16[544,256]{1,0:T(8,128)(2,1)S(1)}, u32[]{:S(2)}, u32[]{:S(2)}) collective-permute-start(bf16[544,256]{1,0:T(8,128)(2,1)S(1)} %get-tuple-element.88), channel_id=1, source_target_pairs={{0,24},{8,16},{16,8},{24,0},{1,25},{9,17},{17,9},{25,1},{2,26},{10... | collective-permute-start | bytes 835592 | tf_op jit(solution)/shard_map/ppermute | solution.py:292
  77.1 9.9 %collective-permute-start.17 = (bf16[512,256]{1,0:T(8,128)(2,1)S(1)}, bf16[512,256]{1,0:T(8,128)(2,1)S(1)}, u32[]{:S(2)}, u32[]{:S(2)}) collective-permute-start(bf16[512,256]{1,0:T(8,128)(2,1)S(1)} %get-tuple-element.82.refs_0_), channel_id=1, source_target_pairs={{0,4},{1,5},{2,6},{3,7},{4,0},{5,1},{6,2},{7,3},{8,12},{9,13},{10,... | collective-permute-start | bytes 786440 | tf_op jit(solution)/shard_map/ppermute | solution.py:292
  77.1 9.9 %collective-permute-start.16 = (bf16[512,256]{1,0:T(8,128)(2,1)S(1)}, bf16[512,256]{1,0:T(8,128)(2,1)S(1)}, u32[]{:S(2)}, u32[]{:S(2)}) collective-permute-start(bf16[512,256]{1,0:T(8,128)(2,1)S(1)} %get-tuple-element.82.refs_0_), channel_id=1, source_target_pairs={{0,2},{1,3},{2,0},{3,1},{4,6},{5,7},{6,4},{7,5},{8,10},{9,11},{10,... | collective-permute-start | bytes 786440 | tf_op jit(solution)/shard_map/ppermute | solution.py:292
  90.7 12.5 %collective-permute-start.24 = (bf16[512,256]{1,0:T(8,128)(2,1)S(1)}, bf16[512,256]{1,0:T(8,128)(2,1)S(1)}, u32[]{:S(2)}, u32[]{:S(2)}) collective-permute-start(bf16[512,256]{1,0:T(8,128)(2,1)S(1)} %get-tuple-element.90.refs_0_), channel_id=1, source_target_pairs={{0,6},{1,7},{2,4},{3,5},{4,2},{5,3},{6,0},{7,1},{8,14},{9,15},{10,... | collective-permute-start | bytes 786440 | tf_op jit(solution)/shard_map/ppermute | solution.py:292
  98.9 16.0 %collective-permute-start.25 = (bf16[544,256]{1,0:T(8,128)(2,1)S(1)}, bf16[544,256]{1,0:T(8,128)(2,1)S(1)}, u32[]{:S(2)}, u32[]{:S(2)}) collective-permute-start(bf16[544,256]{1,0:T(8,128)(2,1)S(1)} %get-tuple-element.93), channel_id=1, source_target_pairs={{0,8},{8,0},{16,24},{24,16},{1,9},{9,1},{17,25},{25,17},{2,10},{10... | collective-permute-start | bytes 835592 | tf_op jit(solution)/shard_map/ppermute | solution.py:292
  100.3 8.6 %collective-permute-start.23 = (bf16[512,256]{1,0:T(8,128)(2,1)S(1)}, bf16[512,256]{1,0:T(8,128)(2,1)S(1)}, u32[]{:S(2)}, u32[]{:S(2)}) collective-permute-start(bf16[512,256]{1,0:T(8,128)(2,1)S(1)} %get-tuple-element.90.refs_0_), channel_id=1, source_target_pairs={{0,4},{1,5},{2,6},{3,7},{4,0},{5,1},{6,2},{7,3},{8,12},{9,13},{10,... | collective-permute-start | bytes 786440 | tf_op jit(solution)/shard_map/ppermute | solution.py:292
  100.4 9.2 %collective-permute-start.22 = (bf16[512,256]{1,0:T(8,128)(2,1)S(1)}, bf16[512,256]{1,0:T(8,128)(2,1)S(1)}, u32[]{:S(2)}, u32[]{:S(2)}) collective-permute-start(bf16[512,256]{1,0:T(8,128)(2,1)S(1)} %get-tuple-element.90.refs_0_), channel_id=1, source_target_pairs={{0,2},{1,3},{2,0},{3,1},{4,6},{5,7},{6,4},{7,5},{8,10},{9,11},{10,... | collective-permute-start | bytes 786440 | tf_op jit(solution)/shard_map/ppermute | solution.py:292
  101.0 15.0 %collective-permute-start.26 = (bf16[544,256]{1,0:T(8,128)(2,1)S(1)}, bf16[544,256]{1,0:T(8,128)(2,1)S(1)}, u32[]{:S(2)}, u32[]{:S(2)}) collective-permute-start(bf16[544,256]{1,0:T(8,128)(2,1)S(1)} %get-tuple-element.94), channel_id=1, source_target_pairs={{0,16},{8,24},{16,0},{24,8},{1,17},{9,25},{17,1},{25,9},{2,18},{10... | collective-permute-start | bytes 835592 | tf_op jit(solution)/shard_map/ppermute | solution.py:292
  103.2 12.8 %collective-permute-start.27 = (bf16[544,256]{1,0:T(8,128)(2,1)S(1)}, bf16[544,256]{1,0:T(8,128)(2,1)S(1)}, u32[]{:S(2)}, u32[]{:S(2)}) collective-permute-start(bf16[544,256]{1,0:T(8,128)(2,1)S(1)} %get-tuple-element.95), channel_id=1, source_target_pairs={{0,24},{8,16},{16,8},{24,0},{1,25},{9,17},{17,9},{25,1},{2,26},{10... | collective-permute-start | bytes 835592 | tf_op jit(solution)/shard_map/ppermute | solution.py:292
  112.5 6.6 %collective-permute-start.28 = (bf16[544,256]{1,0:T(8,128)(2,1)S(1)}, bf16[544,256]{1,0:T(8,128)(2,1)S(1)}, u32[]{:S(2)}, u32[]{:S(2)}) collective-permute-start(bf16[544,256]{1,0:T(8,128)(2,1)S(1)} %get-tuple-element.99), channel_id=1, source_target_pairs={{0,8},{8,0},{16,24},{24,16},{1,9},{9,1},{17,25},{25,17},{2,10},{10... | collective-permute-start | bytes 835592 | tf_op jit(solution)/shard_map/ppermute | solution.py:292
  113.3 8.6 %collective-permute-start.29 = (bf16[544,256]{1,0:T(8,128)(2,1)S(1)}, bf16[544,256]{1,0:T(8,128)(2,1)S(1)}, u32[]{:S(2)}, u32[]{:S(2)}) collective-permute-start(bf16[544,256]{1,0:T(8,128)(2,1)S(1)} %get-tuple-element.100), channel_id=1, source_target_pairs={{0,16},{8,24},{16,0},{24,8},{1,17},{9,25},{17,1},{25,9},{2,18},{10... | collective-permute-start | bytes 835592 | tf_op jit(solution)/shard_map/ppermute | solution.py:292
  114.8 8.2 %collective-permute-start.30 = (bf16[544,256]{1,0:T(8,128)(2,1)S(1)}, bf16[544,256]{1,0:T(8,128)(2,1)S(1)}, u32[]{:S(2)}, u32[]{:S(2)}) collective-permute-start(bf16[544,256]{1,0:T(8,128)(2,1)S(1)} %get-tuple-element.101), channel_id=1, source_target_pairs={{0,24},{8,16},{16,8},{24,0},{1,25},{9,17},{17,9},{25,1},{2,26},{10... | collective-permute-start | bytes 835592 | tf_op jit(solution)/shard_map/ppermute | solution.py:292
  116.8 7.1 %collective-permute-start.31 = (f32[256,256]{1,0:T(8,128)S(1)}, f32[256,256]{1,0:T(8,128)S(1)}, u32[]{:S(2)}, u32[]{:S(2)}) collective-permute-start(f32[256,256]{1,0:T(8,128)S(1)} %get-tuple-element.110), channel_id=1, source_target_pairs={{0,1},{1,0},{2,3},{3,2},{4,5},{5,4},{6,7},{7,6},{8,9},{9,8},{10,11... | collective-permute-start | bytes 786440 | tf_op jit(solution)/shard_map/ppermute | solution.py:292
  123.8 1.6 %collective-permute-start.32 = (f32[256,256]{1,0:T(8,128)S(1)}, f32[256,256]{1,0:T(8,128)S(1)}, u32[]{:S(2)}, u32[]{:S(2)}) collective-permute-start(f32[256,256]{1,0:T(8,128)S(1)} %get-tuple-element.112), channel_id=1, source_target_pairs={{0,1},{1,0},{2,3},{3,2},{4,5},{5,4},{6,7},{7,6},{8,9},{9,8},{10,11... | collective-permute-start | bytes 786440 | tf_op jit(solution)/shard_map/ppermute | solution.py:292
  (5 other events, 22.8 us)
